TPU v7x, 32 devices: a whole 2x2x4 slice. The times are simulated.
32 devices in a mesh: grp: 4 (over z), gx: 2 (over y), gy: 4 (over x, core).
Axes of the slice: x: 2, y: 2, z: 4, core: 2. Of those that a mesh axis runs over, the one named last changes fastest.
Arguments:
- populations: float32 [27, 8, 32, 512], P(None, 'gx', 'gy', 'grp'), may hold values from 0 to 1, as said below
- thermal: float32 [7, 8, 32, 512], P(None, ('gx', 'grp'), 'gy'), may hold values from 0 to 1, as said below
- velocity_prev: float32 [3, 8, 32, 512], P(None, 'gx', 'gy', 'grp'), may hold values from -0.3 to 0.3
- solid: int32 [8, 32, 512], P('gx', 'gy', 'grp'), may hold values 0 or 1
- phase_ids: int32 [8, 32, 512], P(('gx', 'grp'), 'gy'), may hold values from 0 to 3
- conductivity: float32 [4], replicated, may hold values from 0.02 to 0.3
- rates: float32 [27], replicated, may hold values from 0.7 to 1.7
Outputs:
- populations_out: float32 [27, 8, 32, 512], P(None, 'gx', 'gy', 'grp')
- thermal_out: float32 [7, 8, 32, 512], P(None, ('gx', 'grp'), 'gy')
Inputs may be any that keep to these rules, and one draw needn't show every extreme that they name: `populations`: positive. `thermal`: positive.
All inputs are finite; a program needn't handle non-finite values. No bound on the sum of `solid` on one device may be relied on, other than what follows from the above.
Results may differ from a plain program's by a relative error of at most 0.0001.
Values sent between devices are 32-bit elements; how exact they have to be, the bound alone decides.
No kernel may reach another device: no remote copies, remote signals or barrier semaphores. Data moves between devices by JAX's collectives and lax.ppermute only.
A program may use at most 64 MiB of HBM per device.

v0:
```python
import jax
import jax.numpy as jnp
import numpy as np
from jax import lax
from jax.experimental import pallas as pl
from jax.experimental.pallas import tpu as pltpu
from jax.sharding import PartitionSpec as P

STEPS = 4
WINDOWS = 2


HIGHEST = lax.Precision.HIGHEST
BUOYANCY = 0.03
REFERENCE_HEAT = 1.0
OFFSET_TABLE = [(number // 9 - 1, number // 3 % 3 - 1, number % 3 - 1) for number in range(27)]
LATTICE_WEIGHTS = np.array(
    [
        np.prod([2.0 / 3.0 if component == 0 else 1.0 / 6.0 for component in triple])
        for triple in OFFSET_TABLE
    ]
)
VANDERMONDE = np.array([[1.0, 1.0, 1.0], [-1.0, 0.0, 1.0], [1.0, 0.0, 1.0]])
VANDER_INVERSE = np.array([[0.0, -0.5, 0.5], [1.0, 0.0, -1.0], [0.0, 0.5, 0.5]])
MOMENT_MATRIX = np.kron(np.kron(VANDERMONDE, VANDERMONDE), VANDERMONDE)
MOMENT_INVERSE = np.kron(np.kron(VANDER_INVERSE, VANDER_INVERSE), VANDER_INVERSE)
RELAXED = np.array([0.0 if number in (0, 1, 3, 9) else 1.0 for number in range(27)])
SUMMING = np.concatenate([np.ones((1, 27)), 1.0 * np.array(OFFSET_TABLE).T], axis=0)
HEAT_WEIGHTS = np.array([0.25] + [0.125] * 6)


def from_behind(value, axis, steps):
    count = lax.axis_size(axis)
    pairs = [(source, (source + steps) % count) for source in range(count)]
    return lax.ppermute(value, axis, pairs)


def extended(cells, sides, width):
    for axis, dim in sides:
        count = lax.axis_size(axis)
        head = lax.slice_in_dim(cells, 0, width, axis=dim)
        tail = lax.slice_in_dim(cells, cells.shape[dim] - width, cells.shape[dim], axis=dim)
        cells = jnp.concatenate(
            [
                lax.ppermute(tail, axis, [(i, (i + 1) % count) for i in range(count)]),
                cells,
                lax.ppermute(head, axis, [((i + 1) % count, i) for i in range(count)]),
            ],
            axis=dim,
        )
    return cells


def flow_state(flat, heat_flat):
    sums = jnp.dot(jnp.asarray(SUMMING, jnp.float32), flat, precision=HIGHEST)
    density = sums[0]
    force = BUOYANCY * (heat_flat - REFERENCE_HEAT)
    speed = jnp.stack([sums[1], sums[2], sums[3] + 0.5 * force]) / density
    return (density, force, speed)


def collide(popul, heat, rates):
    flat = popul.reshape(27, -1)
    density, force, speed = flow_state(flat, heat.reshape(-1))
    along = jnp.dot(jnp.asarray(SUMMING[1:].T, jnp.float32), speed, precision=HIGHEST)
    square = jnp.sum(speed * speed, axis=0)
    balance = (
        density
        * jnp.asarray(LATTICE_WEIGHTS, jnp.float32)[:, None]
        * (1.0 + 3.0 * along + 4.5 * along * along - 1.5 * square)
    )
    scaled = (
        jnp.asarray(MOMENT_INVERSE, jnp.float32)
        * (rates * jnp.asarray(RELAXED, jnp.float32))[None, :]
    )
    relax = jnp.dot(scaled, jnp.asarray(MOMENT_MATRIX, jnp.float32), precision=HIGHEST)
    post = (
        flat
        - jnp.dot(relax, flat - balance, precision=HIGHEST)
        + jnp.asarray(MOMENT_INVERSE[:, 1], jnp.float32)[:, None] * force[None, :]
    )
    return post.reshape(popul.shape)


def flow_speed(popul, heat, solid):
    density, force, speed = flow_state(popul.reshape(27, -1), heat.reshape(-1))
    return jnp.where(solid[None] == 0, speed.reshape((3,) + solid.shape), 0.0)


def heat_collide(heat_pops, speed, relax_time):
    total = jnp.sum(heat_pops, axis=0)
    still = jnp.zeros_like(speed[0])
    along = jnp.stack([still, speed[0], -speed[0], speed[1], -speed[1], speed[2], -speed[2]])
    balance = (
        jnp.asarray(HEAT_WEIGHTS, jnp.float32)[:, None, None, None]
        * total[None]
        * (1.0 + 4.0 * along)
    )
    return heat_pops - (heat_pops - balance) / relax_time[None]


def relaxation(phase_ids, conductivity):
    levels = jnp.arange(conductivity.shape[0], dtype=jnp.int32)
    chosen = jnp.sum(
        jnp.where(
            phase_ids[None] == levels[:, None, None, None], conductivity[:, None, None, None], 0.0
        ),
        axis=0,
    )
    return 0.5 + 4.0 * chosen


def inner_window(padded, triple, sizes):
    return padded[
        1 - triple[0] : 1 - triple[0] + sizes[0],
        1 - triple[1] : 1 - triple[1] + sizes[1],
        1 - triple[2] : 1 - triple[2] + sizes[2],
    ]


def advance(grid, axis_number, send_up, send_down):
    space = 3 + axis_number
    length = grid.shape[space]
    rising = lax.index_in_dim(grid, 2, axis_number, keepdims=True)
    resting = lax.index_in_dim(grid, 1, axis_number, keepdims=True)
    falling = lax.index_in_dim(grid, 0, axis_number, keepdims=True)
    from_below = send_up(lax.slice_in_dim(rising, length - 1, length, axis=space))
    from_above = send_down(lax.slice_in_dim(falling, 0, 1, axis=space))
    rising = jnp.concatenate(
        [from_below, lax.slice_in_dim(rising, 0, length - 1, axis=space)], axis=space
    )
    falling = jnp.concatenate(
        [lax.slice_in_dim(falling, 1, length, axis=space), from_above], axis=space
    )
    return jnp.concatenate([falling, resting, rising], axis=axis_number)


def flow_arrivals(post):
    sizes = post.shape[1:]
    grid = post.reshape((3, 3, 3) + sizes)
    grid = advance(
        grid,
        0,
        lambda plane: from_behind(plane, "gx", 1),
        lambda plane: from_behind(plane, "gx", -1),
    )
    grid = advance(
        grid,
        1,
        lambda plane: from_behind(plane, "gy", 1),
        lambda plane: from_behind(plane, "gy", -1),
    )
    grid = advance(
        grid,
        2,
        lambda plane: from_behind(plane, "grp", 1),
        lambda plane: from_behind(plane, "grp", -1),
    )
    return grid.reshape(post.shape)


def stream_heat(post, grp_index, last_grp):
    length = post.shape[1]
    size_y = post.shape[2]
    eastward = post[1]
    westward = post[2]
    lower_first = from_behind(eastward, "grp", 1)
    lower_second = from_behind(lower_first, "gx", 1)
    entering = jnp.where(grp_index == 0, lower_second, lower_first)
    eastward = jnp.concatenate([entering, eastward[: length - 1]], axis=0)
    upper_first = from_behind(westward, "grp", -1)
    upper_second = from_behind(upper_first, "gx", -1)
    entering = jnp.where(grp_index == last_grp, upper_second, upper_first)
    westward = jnp.concatenate([westward[1:], entering], axis=0)
    sides = extended(post[3:5], (("gy", 2),), 1)
    northward = sides[0, :, 0:size_y]
    southward = sides[1, :, 2 : size_y + 2]
    upward = jnp.roll(post[5], 1, axis=2)
    downward = jnp.roll(post[6], -1, axis=2)
    return jnp.stack([post[0], eastward, westward, northward, southward, upward, downward])


def on_device(populations, thermal, velocity_prev, solid, phase_ids, conductivity, rates):
    padded_solid = extended(solid, (("grp", 2), ("gx", 0), ("gy", 1)), 1)
    sizes = solid.shape
    blocked = jnp.stack(
        [inner_window(padded_solid, OFFSET_TABLE[number], sizes) != 0 for number in range(27)]
    )
    fluid_cells = (solid == 0)[None]
    grp_index = lax.axis_index("grp")
    last_grp = lax.axis_size("grp") - 1
    relax_time = relaxation(phase_ids, conductivity)
    speed_brick = velocity_prev
    popul = populations
    heat_pops = thermal
    for window_number in range(WINDOWS):
        heat_brick = lax.all_to_all(
            jnp.sum(heat_pops, axis=0), "grp", split_axis=2, concat_axis=0, tiled=True
        )
        speed_column = lax.all_to_all(speed_brick, "grp", split_axis=1, concat_axis=3, tiled=True)
        for step_number in range(STEPS):
            post = collide(popul, heat_brick, rates)
            arrived = flow_arrivals(post)
            popul = jnp.where(fluid_cells, jnp.where(blocked, post[::-1], arrived), popul)
        for step_number in range(STEPS):
            heat_pops = stream_heat(
                heat_collide(heat_pops, speed_column, relax_time), grp_index, last_grp
            )
        if window_number + 1 < WINDOWS:
            speed_brick = flow_speed(popul, heat_brick, solid)
    return (popul, heat_pops)


SUBLANES = 8
LANES = 128
F32 = jnp.float32


class Slab:
    def __init__(self, mesh_shape, flow_block, heat_block):
        self.grp, self.gx, self.gy = (mesh_shape[name] for name in ("grp", "gx", "gy"))
        self.block_x, self.block_y, self.block_z = flow_block
        self.sub = self.gx * self.gy
        self.size_x = self.block_x * self.gx
        self.planes = self.block_z // self.sub
        self.deep = LANES // (self.size_x * self.gy) if self.size_x * self.gy <= LANES else 0
        self.fits = (
            self.block_y == SUBLANES
            and self.block_z == LANES
            and self.block_z % self.sub == 0
            and self.deep >= STEPS
            and self.deep * self.size_x * self.gy == LANES
            and self.planes == self.deep * self.gy
            and 2 * self.block_x == self.sub
            and self.size_x == self.sub
            and self.gx == 2
            and self.block_x == self.grp
            and heat_block == (1, SUBLANES, self.grp * LANES)
            and self.sub & (self.sub - 1) == 0
            and self.gy & (self.gy - 1) == 0
        )
        if self.fits:
            self.tiles = self.planes // self.deep
            self.padded = self.tiles + 2


def lane_index():
    return lax.broadcasted_iota(jnp.int32, (SUBLANES, LANES), 1)


def row_index():
    return lax.broadcasted_iota(jnp.int32, (SUBLANES, LANES), 0)


def lane_roll(value, amount):
    amount = amount % LANES
    return value if amount == 0 else pltpu.roll(value, amount, 1)


def swap_groups(values, group):
    count = len(values)
    lane = lane_index()
    values = list(values)
    bit = 1
    while bit < count:
        low = (lane // (group * bit)) % 2 == 0
        for first in range(count):
            if first & bit == 0:
                a, b = values[first], values[first | bit]
                values[first] = jnp.where(low, a, lane_roll(b, group * bit))
                values[first | bit] = jnp.where(low, lane_roll(a, -group * bit), b)
        bit *= 2
    return values


def pack_in(slab, popul_ref, speed_ref, solid_ref, heat_ref, phase_ref, levels_ref, flow_out, heat_out):
    zero = jnp.zeros((SUBLANES, LANES), F32)

    def field(number, x):
        if number < 27:
            return popul_ref[number, x]
        if number < 30:
            return speed_ref[number - 27, x]
        if number == 30:
            return solid_ref[x].astype(F32)
        return zero

    for pair in range(16):
        sources = [field(2 * pair + h, x) for h in range(2) for x in range(slab.block_x)]
        for target, value in enumerate(swap_groups(sources, slab.planes)):
            flow_out[target, pair] = value
    for part in range(slab.grp):
        span = pl.ds(part * LANES, LANES)
        phase = phase_ref[0, :, span]
        chosen = zero
        for level in range(levels_ref.shape[0]):
            chosen = jnp.where(phase == level, levels_ref[level], chosen)
        sources = [heat_ref[k, 0, :, span] for k in range(7)] + [1.0 / (0.5 + 4.0 * chosen)]
        for target, value in enumerate(swap_groups(sources, slab.planes)):
            heat_out[part * slab.sub + target] = value


HEAT_AT, RATE_AT, SPEED_AT, SOLID_AT, ROWS = 27, 34, 35, 38, 39
MOVING = 34


def row_of_flow(number):
    if number < 27:
        return number
    return SPEED_AT + number - 27 if number < 31 else None


def unpack_in(slab, flow_ref, heat_ref, state_out, low_out, high_out):
    half = slab.block_x * slab.planes
    first_half = lane_index() < half

    def put(row, by_gy):
        for tile, value in enumerate(swap_groups(by_gy, slab.deep)):
            state_out[row, tile] = value
            if tile == 0:
                low_out[row] = value
            if tile == slab.tiles - 1:
                high_out[row] = value

    for pair in range(16):
        firsts, seconds = [], []
        for y in range(slab.gy):
            a, b = flow_ref[y, pair], flow_ref[slab.gy + y, pair]
            firsts.append(jnp.where(first_half, a, lane_roll(b, half)))
            seconds.append(jnp.where(first_half, lane_roll(a, half), b))
        put(row_of_flow(2 * pair), firsts)
        if row_of_flow(2 * pair + 1) is not None:
            put(row_of_flow(2 * pair + 1), seconds)
    columns = []
    for y in range(slab.gy):
        sources = [
            heat_ref[(part * slab.gx + x) * slab.gy + y]
            for x in range(slab.gx)
            for part in range(slab.grp)
        ]
        columns.append(swap_groups(sources, slab.planes))
    for k in range(8):
        put(HEAT_AT + k, [columns[y][k] for y in range(slab.gy)])


def pack_out(slab, take, flow_out, heat_out):
    half = slab.block_x * slab.planes
    first_half = lane_index() < half
    zero = jnp.zeros((SUBLANES, LANES), F32)

    def by_gy(row):
        return swap_groups([take(row, tile) for tile in range(slab.tiles)], slab.deep)

    for pair in range(14):
        firsts = by_gy(2 * pair)
        seconds = by_gy(2 * pair + 1) if 2 * pair + 1 < 27 else [zero] * slab.gy
        for y in range(slab.gy):
            a, b = firsts[y], seconds[y]
            flow_out[y, pair] = jnp.where(first_half, a, lane_roll(b, half))
            flow_out[slab.gy + y, pair] = jnp.where(first_half, lane_roll(a, half), b)
    fields = [by_gy(HEAT_AT + k) for k in range(7)]
    for y in range(slab.gy):
        sources = [fields[k][y] for k in range(7)] + [zero]
        for number, value in enumerate(swap_groups(sources, slab.planes)):
            x, part = number // slab.grp, number % slab.grp
            heat_out[(part * slab.gx + x) * slab.gy + y] = value


def unpack_out(slab, flow_ref, heat_ref, popul_out, thermal_out):
    for pair in range(14):
        sources = [flow_ref[source, pair] for source in range(slab.sub)]
        for number, value in enumerate(swap_groups(sources, slab.planes)):
            field, x = 2 * pair + number // slab.block_x, number % slab.block_x
            if field < 27:
                popul_out[field, x] = value
    for part in range(slab.grp):
        sources = [heat_ref[part * slab.sub + source] for source in range(slab.sub)]
        for k, value in enumerate(swap_groups(sources, slab.planes)[:7]):
            thermal_out[k, 0, :, pl.ds(part * LANES, LANES)] = value


def forward3(values):
    for stride in (9, 3, 1):
        out = [None] * 27
        for n in range(27):
            if n // stride % 3 == 0:
                a, b, c = values[n], values[n + stride], values[n + 2 * stride]
                both = a + c
                out[n], out[n + stride], out[n + 2 * stride] = both + b, c - a, both
        values = out
    return values


def backward3(values):
    for stride in (9, 3, 1):
        out = [None] * 27
        for n in range(27):
            if n // stride % 3 == 0:
                a, b, c = values[n], values[n + stride], values[n + 2 * stride]
                even, odd = 0.5 * c, 0.5 * b
                out[n], out[n + stride], out[n + 2 * stride] = even - odd, a - c, even + odd
        values = out
    return values


def collide_tile(values, force, rate):
    moments = forward3(values)
    density = moments[0]
    jx, jy, jz = moments[9], moments[3], moments[1] + 0.5 * force
    inverse = 1.0 / density
    flux = (jx, jy, jz)
    u = tuple(j * inverse for j in flux)
    third = 1.0 / 3.0
    base = {0: density}
    for k in (1, 2, 3):
        base[k] = density * third**k
    squares = [flux[d] * u[d] for d in range(3)]
    square_at = {}
    scaled = {}

    def scale(key, value, count):
        if count == 0:
            return value
        if (key, count) not in scaled:
            scaled[key, count] = value * third**count
        return scaled[key, count]

    cross = {(0, 1): jx * u[1], (0, 2): jx * u[2], (1, 2): jy * u[2]}
    out = [None] * 27
    for n in range(27):
        powers = (n // 9, n // 3 % 3, n % 3)
        if n in (0, 3, 9):
            out[n] = moments[n]
            continue
        if n == 1:
            out[n] = moments[n] + force
            continue
        odd = tuple(d for d in range(3) if powers[d] == 1)
        even = tuple(d for d in range(3) if powers[d] == 2)
        count = len(even)
        if len(odd) == 3:
            out[n] = moments[n] - rate(n) * moments[n]
            continue
        if len(odd) == 0:
            if even not in square_at:
                total = squares[even[0]]
                for d in even[1:]:
                    total = total + squares[d]
                square_at[even] = base[count] + (total * (3.0 * third**count) if count > 1 else total)
            level = square_at[even]
        elif len(odd) == 1:
            level = scale(odd, flux[odd[0]], count)
        else:
            level = scale(odd, cross[odd], count)
        out[n] = moments[n] - rate(n) * (moments[n] - level)
    return backward3(out)


def shifters(slab):
    lane, row = lane_index(), row_index()
    per_x = slab.gy * slab.deep
    in_z = lane % slab.deep
    in_y = (lane // slab.deep) % slab.gy
    z_edge = {1: in_z == 0, -1: in_z == slab.deep - 1}
    y_edge = {1: in_y == 0, -1: in_y == slab.gy - 1}
    row_edge = {1: row == 0, -1: row == SUBLANES - 1}

    def along_x(value, step):
        return lane_roll(value, step * per_x)

    def along_y(value, step):
        turned = pltpu.roll(value, step % SUBLANES, 0)
        near = lane_roll(turned, step * slab.deep)
        far = lane_roll(turned, step * (slab.deep - per_x))
        return jnp.where(row_edge[step], jnp.where(y_edge[step], far, near), turned)

    def along_z(value, beside, step):
        return jnp.where(z_edge[step], lane_roll(beside, step * (1 - slab.deep)), lane_roll(value, step))

    return along_x, along_y, along_z


HEAT_OFFSETS = [(0, 0, 0), (1, 0, 0), (-1, 0, 0), (0, 1, 0), (0, -1, 0), (0, 0, 1), (0, 0, -1)]


def run_steps(slab, rates_ref, state, post, force_ref, rate_ref, speed_ref, solid_ref):
    last = slab.padded - 1

    def collide_one(tile, _):
        values = [state[n, tile] for n in range(27)]
        solid = solid_ref[tile] != 0.0
        moved = collide_tile(values, force_ref[tile], lambda n: rates_ref[n])
        for n in range(27):
            post[n, tile] = jnp.where(solid, jnp.nan, moved[n])
        heat = [state[HEAT_AT + k, tile] for k in range(7)]
        total = heat[0]
        for k in range(1, 7):
            total = total + heat[k]
        omega = rate_ref[tile]
        side = 0.125 * total
        for k in range(7):
            if k == 0:
                level = 0.25 * total
            else:
                drift = (0.5 * total) * speed_ref[(k - 1) // 2, tile]
                level = side + drift if k % 2 == 1 else side - drift
            post[HEAT_AT + k, tile] = heat[k] - (heat[k] - level) * omega
        return 0

    def stream_one(tile, _):
        along_x, along_y, along_z = shifters(slab)
        before = jnp.where(tile == 0, last, tile - 1)
        after = jnp.where(tile == last, 0, tile + 1)
        solid = solid_ref[tile] != 0.0

        def arrive(row, offset):
            value = post[row, tile]
            if offset[2] != 0:
                value = along_z(value, post[row, before if offset[2] == 1 else after], offset[2])
            if offset[1] != 0:
                value = along_y(value, offset[1])
            if offset[0] != 0:
                value = along_x(value, offset[0])
            return value

        for n in range(27):
            value = arrive(n, OFFSET_TABLE[n])
            value = jnp.where(value != value, post[26 - n, tile], value)
            state[n, tile] = jnp.where(solid, state[n, tile], value)
        for k in range(7):
            state[HEAT_AT + k, tile] = arrive(HEAT_AT + k, HEAT_OFFSETS[k])
        return 0

    def step(number, _):
        lax.fori_loop(0, slab.padded, collide_one, 0)
        lax.fori_loop(0, slab.padded, stream_one, 0)
        return 0

    lax.fori_loop(0, STEPS, step, 0)


def heat_force(state, tile):
    total = state[HEAT_AT, tile]
    for k in range(1, 7):
        total = total + state[HEAT_AT + k, tile]
    return BUOYANCY * (total - REFERENCE_HEAT)


def first_window(slab, rates_ref, own_ref, low_ref, high_ref, own_out, low_out, high_out, keep_out, state, post, speed):
    def gather(row, tile):
        if tile == 0:
            return low_ref[row]
        if tile == slab.padded - 1:
            return high_ref[row]
        return own_ref[row, tile - 1]

    for tile in range(slab.padded):
        for row in range(MOVING):
            state[row, tile] = gather(row, tile)
        for d in range(3):
            speed[d, tile] = gather(SPEED_AT + d, tile)
        keep_out[0, tile] = gather(RATE_AT, tile)
        keep_out[1, tile] = gather(SOLID_AT, tile)
        keep_out[2, tile] = heat_force(state, tile)
    run_steps(slab, rates_ref, state, post, keep_out.at[2], keep_out.at[0], speed, keep_out.at[1])
    for row in range(MOVING):
        for tile in range(slab.tiles):
            own_out[row, tile] = state[row, tile + 1]
        low_out[row] = state[row, 1]
        high_out[row] = state[row, slab.tiles]


def next_state(slab, own_ref, low_ref, high_ref, keep_ref, state, speed, force):
    for tile in range(slab.padded):
        for row in range(MOVING):
            if tile == 0:
                state[row, tile] = low_ref[row]
            elif tile == slab.padded - 1:
                state[row, tile] = high_ref[row]
            else:
                state[row, tile] = own_ref[row, tile - 1]
        values = [state[n, tile] for n in range(27)]
        total = values[0]
        for n in range(1, 27):
            total = total + values[n]
        sums = []
        for d in range(3):
            plus, minus = None, None
            for n in range(27):
                part = OFFSET_TABLE[n][d]
                if part == 1:
                    plus = values[n] if plus is None else plus + values[n]
                if part == -1:
                    minus = values[n] if minus is None else minus + values[n]
            sums.append(plus - minus)
        sums[2] = sums[2] + 0.5 * keep_ref[2, tile]
        solid = keep_ref[1, tile] != 0.0
        for d in range(3):
            speed[d, tile] = jnp.where(solid, 0.0, sums[d] / total)
        force[tile] = heat_force(state, tile)


def last_window(slab, rates_ref, own_ref, low_ref, high_ref, keep_ref, flow_out, heat_out, state, post, speed, force):
    next_state(slab, own_ref, low_ref, high_ref, keep_ref, state, speed, force)
    run_steps(slab, rates_ref, state, post, force, keep_ref.at[0], speed, keep_ref.at[1])
    pack_out(slab, lambda row, tile: state[row, tile + 1], flow_out, heat_out)


def middle_window(slab, rates_ref, own_ref, low_ref, high_ref, keep_ref, own_out, low_out, high_out, keep_out, state, post, speed):
    for k in range(2):
        for tile in range(slab.padded):
            keep_out[k, tile] = keep_ref[k, tile]
    next_state(slab, own_ref, low_ref, high_ref, keep_ref, state, speed, keep_out.at[2])
    run_steps(slab, rates_ref, state, post, keep_out.at[2], keep_out.at[0], speed, keep_out.at[1])
    for row in range(MOVING):
        for tile in range(slab.tiles):
            own_out[row, tile] = state[row, tile + 1]
        low_out[row] = state[row, 1]
        high_out[row] = state[row, slab.tiles]


def local_call(body, slab, scalars, arrays, outs, scratch=()):
    def kernel(*refs):
        body(slab, *refs)

    return pl.pallas_call(
        kernel,
        out_shape=[jax.ShapeDtypeStruct(shape, F32) for shape in outs],
        in_specs=[pl.BlockSpec(memory_space=pltpu.SMEM)] * len(scalars)
        + [pl.BlockSpec(memory_space=pltpu.VMEM)] * len(arrays),
        out_specs=[pl.BlockSpec(memory_space=pltpu.VMEM)] * len(outs),
        scratch_shapes=[pltpu.VMEM(shape, F32) for shape in scratch],
        compiler_params=pltpu.CompilerParams(vmem_limit_bytes=24 * 1024 * 1024),
    )(*scalars, *arrays)


RING = ("grp", "gx", "gy")


def exchange(low, high, count):
    from_below = lax.ppermute(high, RING, [(i, (i + 1) % count) for i in range(count)])
    from_above = lax.ppermute(low, RING, [((i + 1) % count, i) for i in range(count)])
    return from_below, from_above


def on_slabs(slab, populations, thermal, velocity_prev, solid, phase_ids, conductivity, rates):
    tile = (SUBLANES, LANES)
    count = slab.grp * slab.sub

    def pack_body(slab, levels_ref, popul_ref, speed_ref, solid_ref, heat_ref, phase_ref, flow_out, heat_out):
        pack_in(slab, popul_ref, speed_ref, solid_ref, heat_ref, phase_ref, levels_ref, flow_out, heat_out)

    flow, heat = local_call(
        pack_body,
        slab,
        [conductivity],
        [populations, velocity_prev, solid, thermal, phase_ids],
        [(slab.sub, 16) + tile, (count,) + tile],
    )
    heat = lax.all_to_all(heat, RING, split_axis=0, concat_axis=0, tiled=True)
    flow = lax.all_to_all(flow, ("gx", "gy"), split_axis=0, concat_axis=0, tiled=True)
    own, low, high = local_call(
        unpack_in,
        slab,
        [],
        [flow, heat],
        [(ROWS, slab.tiles) + tile, (ROWS,) + tile, (ROWS,) + tile],
    )
    window_outs = [
        (MOVING, slab.tiles) + tile,
        (MOVING,) + tile,
        (MOVING,) + tile,
        (3, slab.padded) + tile,
    ]
    lattice = (MOVING, slab.padded) + tile
    below, above = exchange(low, high, count)
    own, low, high, keep = local_call(
        first_window,
        slab,
        [rates],
        [own, below, above],
        window_outs,
        [lattice, lattice, (3, slab.padded) + tile],
    )
    for number in range(1, WINDOWS):
        below, above = exchange(low, high, count)
        if number + 1 < WINDOWS:
            own, low, high, keep = local_call(
                middle_window,
                slab,
                [rates],
                [own, below, above, keep],
                window_outs,
                [lattice, lattice, (3, slab.padded) + tile],
            )
        else:
            flow, heat = local_call(
                last_window,
                slab,
                [rates],
                [own, below, above, keep],
                [(slab.sub, 14) + tile, (count,) + tile],
                [lattice, lattice, (3, slab.padded) + tile, (slab.padded,) + tile],
            )
    flow = lax.all_to_all(flow, ("gx", "gy"), split_axis=0, concat_axis=0, tiled=True)
    heat = lax.all_to_all(heat, RING, split_axis=0, concat_axis=0, tiled=True)
    return tuple(
        local_call(unpack_out, slab, [], [flow, heat], [populations.shape, thermal.shape])
    )


def solution(mesh):
    in_specs = (
        P(None, "gx", "gy", "grp"),
        P(None, ("gx", "grp"), "gy", None),
        P(None, "gx", "gy", "grp"),
        P("gx", "gy", "grp"),
        P(("gx", "grp"), "gy", None),
        P(),
        P(),
    )
    out_specs = (P(None, "gx", "gy", "grp"), P(None, ("gx", "grp"), "gy", None))

    def per_device(populations, thermal, *others):
        slab = Slab(mesh.shape, populations.shape[1:], thermal.shape[1:])
        plan = (lambda *arrays: on_slabs(slab, *arrays)) if slab.fits and WINDOWS > 1 else on_device
        return plan(populations, thermal, *others)

    return jax.shard_map(
        per_device, mesh=mesh, in_specs=in_specs, out_specs=out_specs, check_vma=False
    )
```

profile of v0, /device:TPU:0, one launch (start us, length us, event | category | flops | bytes accessed | tf_op | source)
XLA Modules:
  0.0 102.5 jit_solution(16146396549606244661)
XLA Ops:
  0.6 0.0 copy-start
  0.6 1.0 copy-done
  1.6 0.0 copy-start.1
  1.6 0.9 copy-done.1
  2.5 0.0 copy-start.2
  2.5 0.8 copy-done.2
  3.3 0.0 copy-start.3
  3.3 0.7 copy-done.3
  4.1 0.0 copy-start.4
  4.1 0.7 copy-done.4
  4.8 0.0 copy-start.6
  4.8 0.7 copy-done.6
  5.4 2.7 %shard_map.86 = (f32[8,16,8,128]{3,2,1,0:T(8,128)S(1)}, f32[32,8,128]{2,1,0:T(8,128)S(1)}) custom-call(f32[4]{0:T(128)S(1)} %copy-done.6, f32[27,4,8,128]{3,2,1,0:T(8,128)S(1)} %copy-done, f32[3,4,8,128]{3,2,1,0:T(8,128)S(1)} %copy-done.2, s32[4,8,128]{2,1,0:T(8,128)S(1)} %copy-done.3, f32[7,1,8,512]{3,2,1,0:T(8,128)S(1)} %copy-done.1, ...), custom_call_target="tpu_custom_call" | custom-call | tf_op jit(solution)/shard_map/pallas_call | solution.py:626
  8.1 15.3 %all_to_all.20.refs_1_ = f32[32,8,128]{2,1,0:T(8,128)S(1)} all-to-all(f32[32,8,128]{2,1,0:T(8,128)S(1)} %get-tuple-element.14), channel_id=1, replica_groups=mesh['grp'=4,'gx'=2,'gy'=4] {'grp','gx','gy'}, dimensions={0} | all-to-all | bytes 262144 | tf_op jit(solution)/shard_map/all_to_all | solution.py:660
  23.4 12.1 %all_to_all.21.refs_0_ = f32[8,16,8,128]{3,2,1,0:T(8,128)S(1)} all-to-all(f32[8,16,8,128]{3,2,1,0:T(8,128)S(1)} %get-tuple-element.13), channel_id=1, replica_groups=mesh['grp'=4,'gx'=2,'gy'=4] {'gx','gy'}, dimensions={0} | all-to-all | bytes 1048576 | tf_op jit(solution)/shard_map/all_to_all | solution.py:661
  35.6 2.9 %shard_map.87 = (f32[39,4,8,128]{3,2,1,0:T(8,128)S(1)}, f32[39,8,128]{2,1,0:T(8,128)S(1)}, f32[39,8,128]{2,1,0:T(8,128)S(1)}) custom-call(f32[8,16,8,128]{3,2,1,0:T(8,128)S(1)} %all_to_all.21.refs_0_, f32[32,8,128]{2,1,0:T(8,128)S(1)} %all_to_all.20.refs_1_), custom_call_target="tpu_custom_call" | custom-call | tf_op jit(solution)/shard_map/pallas_call | solution.py:626
  38.4 0.1 collective-permute-start
  38.5 0.0 copy-start.5
  38.5 5.3 %collective-permute-start.1 = (f32[39,8,128]{2,1,0:T(8,128)S(1)}, f32[39,8,128]{2,1,0:T(8,128)S(1)}, u32[]{:S(2)}, u32[]{:S(2)}) collective-permute-start(f32[39,8,128]{2,1,0:T(8,128)S(1)} %get-tuple-element.17), channel_id=1, source_target_pairs={{1,0},{2,1},{3,2},{4,3},{5,4},{6,5},{7,6},{8,7},{9,8},{10,9},{11,1... | collective-permute-start | bytes 479240 | tf_op jit(solution)/shard_map/ppermute | solution.py:642
  43.8 3.0 %collective-permute-done.refs_2_ = f32[39,8,128]{2,1,0:T(8,128)S(1)} collective-permute-done((f32[39,8,128]{2,1,0:T(8,128)S(1)}, f32[39,8,128]{2,1,0:T(8,128)S(1)}, u32[]{:S(2)}, u32[]{:S(2)}) %collective-permute-start) | collective-permute-done | bytes 159776 | tf_op jit(solution)/shard_map/ppermute | solution.py:641
  46.8 0.0 collective-permute-done.1.refs_3_
  46.8 0.0 copy-done.5
  46.8 8.7 %shard_map.88 = (f32[34,4,8,128]{3,2,1,0:T(8,128)S(1)}, f32[34,8,128]{2,1,0:T(8,128)S(1)}, f32[34,8,128]{2,1,0:T(8,128)S(1)}, f32[3,6,8,128]{3,2,1,0:T(8,128)S(1)}) custom-call(f32[27]{0:T(128)S(1)} %copy-done.5, f32[39,4,8,128]{3,2,1,0:T(8,128)S(1)} %get-tuple-element.15.refs_1_, f32[39,8,128]{2,1,0:T(8,128)S(1)} %collective-permute-done.refs_2_, ...), custom_call_target="tpu_custom_call" | custom-call | tf_op jit(solution)/shard_map/pallas_call | solution.py:626
  55.5 0.1 collective-permute-start.2
  55.5 5.4 %collective-permute-start.3 = (f32[34,8,128]{2,1,0:T(8,128)S(1)}, f32[34,8,128]{2,1,0:T(8,128)S(1)}, u32[]{:S(2)}, u32[]{:S(2)}) collective-permute-start(f32[34,8,128]{2,1,0:T(8,128)S(1)} %get-tuple-element.20), channel_id=1, source_target_pairs={{1,0},{2,1},{3,2},{4,3},{5,4},{6,5},{7,6},{8,7},{9,8},{10,9},{11,1... | collective-permute-start | bytes 417800 | tf_op jit(solution)/shard_map/ppermute | solution.py:642
  60.9 2.7 %collective-permute-done.2.refs_2_ = f32[34,8,128]{2,1,0:T(8,128)S(1)} collective-permute-done((f32[34,8,128]{2,1,0:T(8,128)S(1)}, f32[34,8,128]{2,1,0:T(8,128)S(1)}, u32[]{:S(2)}, u32[]{:S(2)}) %collective-permute-start.2) | collective-permute-done | bytes 139296 | tf_op jit(solution)/shard_map/ppermute | solution.py:641
  63.6 0.0 collective-permute-done.3.refs_3_
  63.6 11.1 %shard_map.89 = (f32[8,14,8,128]{3,2,1,0:T(8,128)S(1)}, f32[32,8,128]{2,1,0:T(8,128)S(1)}) custom-call(f32[27]{0:T(128)S(1)} %copy-done.5, f32[34,4,8,128]{3,2,1,0:T(8,128)S(1)} %get-tuple-element.18.refs_1_, f32[34,8,128]{2,1,0:T(8,128)S(1)} %collective-permute-done.2.refs_2_, f32[34,8,128]{2,1,0:T(8,128)S(1)} %collective-permute-done.3.refs_3_, ...), custom_call_target="tpu_custom_call" | custom-call | tf_op jit(solution)/shard_map/pallas_call | solution.py:626
  74.7 13.8 %all_to_all.22.refs_1_ = f32[32,8,128]{2,1,0:T(8,128)S(1)} all-to-all(f32[32,8,128]{2,1,0:T(8,128)S(1)} %get-tuple-element.23), channel_id=1, replica_groups=mesh['grp'=4,'gx'=2,'gy'=4] {'grp','gx','gy'}, dimensions={0} | all-to-all | bytes 262144 | tf_op jit(solution)/shard_map/all_to_all | solution.py:706
  88.5 11.4 %all_to_all.23.refs_0_ = f32[8,14,8,128]{3,2,1,0:T(8,128)S(1)} all-to-all(f32[8,14,8,128]{3,2,1,0:T(8,128)S(1)} %get-tuple-element.22), channel_id=1, replica_groups=mesh['grp'=4,'gx'=2,'gy'=4] {'gx','gy'}, dimensions={0} | all-to-all | bytes 917504 | tf_op jit(solution)/shard_map/all_to_all | solution.py:705
  100.0 2.5 %shard_map.90 = (f32[27,4,8,128]{3,2,1,0:T(8,128)}, f32[7,1,8,512]{3,2,1,0:T(8,128)}) custom-call(f32[8,14,8,128]{3,2,1,0:T(8,128)S(1)} %all_to_all.23.refs_0_, f32[32,8,128]{2,1,0:T(8,128)S(1)} %all_to_all.22.refs_1_), custom_call_target="tpu_custom_call" | custom-call | tf_op jit(solution)/shard_map/pallas_call | solution.py:626
Async XLA Ops:
  0.6 1.0 copy-start
  1.6 0.9 copy-start.1
  2.5 0.8 copy-start.2
  3.3 0.7 copy-start.3
  4.1 0.7 copy-start.4
  4.8 0.7 copy-start.6
  38.4 8.3 %collective-permute-start = (f32[39,8,128]{2,1,0:T(8,128)S(1)}, f32[39,8,128]{2,1,0:T(8,128)S(1)}, u32[]{:S(2)}, u32[]{:S(2)}) collective-permute-start(f32[39,8,128]{2,1,0:T(8,128)S(1)} %get-tuple-element.16), channel_id=1, source_target_pairs={{0,1},{1,2},{2,3},{3,4},{4,5},{5,6},{6,7},{7,8},{8,9},{9,10},{10,1... | collective-permute-start | bytes 479240 | tf_op jit(solution)/shard_map/ppermute | solution.py:641
  38.5 8.3 %copy-start.5 = (f32[27]{0:T(128)S(1)}, f32[27]{0:T(128)}, u32[]{:S(2)}) copy-start(f32[27]{0:T(128)} %refs_0_.5) | copy-start | bytes 328
  38.5 8.3 %collective-permute-start.1 = (f32[39,8,128]{2,1,0:T(8,128)S(1)}, f32[39,8,128]{2,1,0:T(8,128)S(1)}, u32[]{:S(2)}, u32[]{:S(2)}) collective-permute-start(f32[39,8,128]{2,1,0:T(8,128)S(1)} %get-tuple-element.17), channel_id=1, source_target_pairs={{1,0},{2,1},{3,2},{4,3},{5,4},{6,5},{7,6},{8,7},{9,8},{10,9},{11,1... | collective-permute-start | bytes 479240 | tf_op jit(solution)/shard_map/ppermute | solution.py:642
  55.5 8.1 %collective-permute-start.2 = (f32[34,8,128]{2,1,0:T(8,128)S(1)}, f32[34,8,128]{2,1,0:T(8,128)S(1)}, u32[]{:S(2)}, u32[]{:S(2)}) collective-permute-start(f32[34,8,128]{2,1,0:T(8,128)S(1)} %get-tuple-element.19), channel_id=1, source_target_pairs={{0,1},{1,2},{2,3},{3,4},{4,5},{5,6},{6,7},{7,8},{8,9},{9,10},{10,1... | collective-permute-start | bytes 417800 | tf_op jit(solution)/shard_map/ppermute | solution.py:641
  55.5 8.1 %collective-permute-start.3 = (f32[34,8,128]{2,1,0:T(8,128)S(1)}, f32[34,8,128]{2,1,0:T(8,128)S(1)}, u32[]{:S(2)}, u32[]{:S(2)}) collective-permute-start(f32[34,8,128]{2,1,0:T(8,128)S(1)} %get-tuple-element.20), channel_id=1, source_target_pairs={{1,0},{2,1},{3,2},{4,3},{5,4},{6,5},{7,6},{8,7},{9,8},{10,9},{11,1... | collective-permute-start | bytes 417800 | tf_op jit(solution)/shard_map/ppermute | solution.py:642
where the time goes:
time: 103 us; the launch traced here: 102 us
  blocking collectives  52.7 us (51%)
  Pallas kernels  27.8 us (27%)
  starting transfers between devices  10.8 us (10%)
  waiting for transfers between devices  5.63 us (5%)
  local copies, waits for them, and re-layouts  4.8 us (5%)
    all_to_all x2, blocking collectives, on_slabs(): heat = lax.all_to_all(heat, RING, split_axis=0, concat_axis=0, tiled=True)  29.1 us
    pallas_call x5, Pallas kernels, local_call(): pl.pallas_call(kernel, out_shape=[jax.ShapeDtypeStruct(shape, F32) for sh...  27.8 us
    all_to_all x2, blocking collectives, on_slabs(): lax.all_to_all(flow, ('gx', 'gy'), split_axis=0, concat_axis=0, tiled=True)  23.6 us
    ppermute x2, starting transfers between devices, exchange(): lax.ppermute(low, RING, [((i + 1) % count, i) for i in range(count)])  10.7 us
    ppermute x2, waiting for transfers between devices, exchange(): lax.ppermute(high, RING, [(i, (i + 1) % count) for i in range(count)])  5.63 us
    unnamed x14, local copies, waits for them, and re-layouts  4.8 us
  transfers between devices with their start and end apart: 4, of which 2 were waited for; matrix products, arithmetic and copies ran while one was open for 0% of the time, Pallas kernels for 0%

commit v1 on v0

--- a/solution.py
+++ b/solution.py
@@ -238,10 +238,24 @@
             and heat_block == (1, SUBLANES, self.grp * LANES)
             and self.sub & (self.sub - 1) == 0
             and self.gy & (self.gy - 1) == 0
+            and self.grp & (self.grp - 1) == 0
         )
         if self.fits:
             self.tiles = self.planes // self.deep
             self.padded = self.tiles + 2
+            self.snake = [
+                x * self.gy + (y if x % 2 == 0 else self.gy - 1 - y)
+                for x in range(self.gx)
+                for y in range(self.gy)
+            ]
+            self.ring = [
+                part * self.sub + self.snake[place if part % 2 == 0 else self.sub - 1 - place]
+                for part in range(self.grp)
+                for place in range(self.sub)
+            ]
+
+    def holder(self, place, part):
+        return jnp.where(part % 2 == 0, self.snake[place], self.snake[self.sub - 1 - place])
 
 
 def lane_index():
@@ -273,44 +287,105 @@
     return values
 
 
-def pack_in(slab, popul_ref, speed_ref, solid_ref, heat_ref, phase_ref, levels_ref, flow_out, heat_out):
-    zero = jnp.zeros((SUBLANES, LANES), F32)
-
-    def field(number, x):
-        if number < 27:
-            return popul_ref[number, x]
-        if number < 30:
-            return speed_ref[number - 27, x]
-        if number == 30:
-            return solid_ref[x].astype(F32)
-        return zero
-
-    for pair in range(16):
-        sources = [field(2 * pair + h, x) for h in range(2) for x in range(slab.block_x)]
-        for target, value in enumerate(swap_groups(sources, slab.planes)):
-            flow_out[target, pair] = value
-    for part in range(slab.grp):
-        span = pl.ds(part * LANES, LANES)
+SENT_SPEED, SENT_SOLID, SENT_HEAT, SENT_RATE, SENT = 27, 30, 31, 38, 40
+HEAT_AT, RATE_AT, SPEED_AT, SOLID_AT, ROWS = 27, 34, 35, 38, 39
+MOVING = 34
+
+
+def row_of(number):
+    if number < SENT_SPEED:
+        return number
+    if number < SENT_SOLID:
+        return SPEED_AT + number - SENT_SPEED
+    if number == SENT_SOLID:
+        return SOLID_AT
+    return HEAT_AT + number - SENT_HEAT if number <= SENT_RATE else None
+
+
+def offer_heat(slab, levels_hbm, heat_hbm, phase_hbm, *refs):
+    outs, (levels_ref, heat_ref, phase_ref, sems) = refs[: slab.grp], refs[slab.grp :]
+    copies = [
+        pltpu.make_async_copy(heat_hbm, heat_ref, sems.at[0]),
+        pltpu.make_async_copy(phase_hbm, phase_ref, sems.at[1]),
+        pltpu.make_async_copy(levels_hbm, levels_ref, sems.at[2]),
+    ]
+    for copy in copies:
+        copy.start()
+    for copy in copies:
+        copy.wait()
+    mine = lax.axis_index("grp")
+    for step in range(slab.grp):
+        part = jnp.bitwise_xor(mine, step)
+        span = pl.ds(pl.multiple_of(part * LANES, LANES), LANES)
         phase = phase_ref[0, :, span]
-        chosen = zero
+        chosen = jnp.zeros((SUBLANES, LANES), F32)
         for level in range(levels_ref.shape[0]):
             chosen = jnp.where(phase == level, levels_ref[level], chosen)
-        sources = [heat_ref[k, 0, :, span] for k in range(7)] + [1.0 / (0.5 + 4.0 * chosen)]
-        for target, value in enumerate(swap_groups(sources, slab.planes)):
-            heat_out[part * slab.sub + target] = value
-
-
-HEAT_AT, RATE_AT, SPEED_AT, SOLID_AT, ROWS = 27, 34, 35, 38, 39
-MOVING = 34
-
-
-def row_of_flow(number):
-    if number < 27:
-        return number
-    return SPEED_AT + number - 27 if number < 31 else None
-
-
-def unpack_in(slab, flow_ref, heat_ref, state_out, low_out, high_out):
+        for k in range(7):
+            outs[step][k] = heat_ref[k, 0, :, span]
+        outs[step][7] = 1.0 / (0.5 + 4.0 * chosen)
+
+
+def pack_flow(
+    slab, popul_hbm, speed_hbm, solid_hbm, sent, flags, popul_ref, speed_ref, solid_ref, sems
+):
+    half = 14
+    copies = [
+        pltpu.make_async_copy(popul_hbm.at[pl.ds(0, half)], popul_ref.at[pl.ds(0, half)], sems.at[0]),
+        pltpu.make_async_copy(
+            popul_hbm.at[pl.ds(half, 27 - half)], popul_ref.at[pl.ds(half, 27 - half)], sems.at[1]
+        ),
+        pltpu.make_async_copy(speed_hbm, speed_ref, sems.at[2]),
+        pltpu.make_async_copy(solid_hbm, solid_ref, sems.at[3]),
+    ]
+    for copy in copies:
+        copy.start()
+    mine = lax.axis_index("grp")
+    holders = [slab.holder(place, mine) for place in range(slab.sub)]
+
+    def field(number, x):
+        if number < SENT_SPEED:
+            return popul_ref[number, x]
+        return speed_ref[number - SENT_SPEED, x]
+
+    copies[0].wait()
+    for pair in range(SENT_SOLID // 2):
+        if 2 * pair == half:
+            copies[1].wait()
+        if pair == SENT_SPEED // 2:
+            copies[2].wait()
+            copies[3].wait()
+        sources = [field(2 * pair + h, x) for h in range(2) for x in range(slab.block_x)]
+        for place, value in enumerate(swap_groups(sources, slab.planes)):
+            sent[holders[place], pair] = value
+    for x in range(slab.block_x):
+        flags[x] = solid_ref[x].astype(F32)
+
+
+def pack_heat(slab, sent_in, flags, *refs):
+    parts, (sent, held, packed, sem) = refs[: slab.grp], refs[slab.grp :]
+    mine = lax.axis_index("grp")
+    holders = [slab.holder(place, mine) for place in range(slab.sub)]
+    for step in range(slab.grp):
+        held[jnp.bitwise_xor(mine, step)] = parts[step][...]
+    zero = jnp.zeros((SUBLANES, LANES), F32)
+    first = SENT_SOLID // 2
+
+    def field(number, x):
+        if number == SENT_SOLID:
+            return flags[x]
+        return held[x, number - SENT_HEAT] if number <= SENT_RATE else zero
+
+    for pair in range(first, SENT // 2):
+        sources = [field(2 * pair + h, x) for h in range(2) for x in range(slab.block_x)]
+        for place, value in enumerate(swap_groups(sources, slab.planes)):
+            packed[holders[place], pair - first] = value
+    copy = pltpu.make_async_copy(packed, sent.at[:, pl.ds(first, SENT // 2 - first)], sem)
+    copy.start()
+    copy.wait()
+
+
+def unpack_in(slab, came, state_out, low_out, high_out):
     half = slab.block_x * slab.planes
     first_half = lane_index() < half
 
@@ -322,61 +397,65 @@
             if tile == slab.tiles - 1:
                 high_out[row] = value
 
-    for pair in range(16):
+    for pair in range(SENT // 2):
         firsts, seconds = [], []
         for y in range(slab.gy):
-            a, b = flow_ref[y, pair], flow_ref[slab.gy + y, pair]
+            a, b = came[y, pair], came[slab.gy + y, pair]
             firsts.append(jnp.where(first_half, a, lane_roll(b, half)))
             seconds.append(jnp.where(first_half, lane_roll(a, half), b))
-        put(row_of_flow(2 * pair), firsts)
-        if row_of_flow(2 * pair + 1) is not None:
-            put(row_of_flow(2 * pair + 1), seconds)
-    columns = []
-    for y in range(slab.gy):
-        sources = [
-            heat_ref[(part * slab.gx + x) * slab.gy + y]
-            for x in range(slab.gx)
-            for part in range(slab.grp)
-        ]
-        columns.append(swap_groups(sources, slab.planes))
-    for k in range(8):
-        put(HEAT_AT + k, [columns[y][k] for y in range(slab.gy)])
-
-
-def pack_out(slab, take, flow_out, heat_out):
+        put(row_of(2 * pair), firsts)
+        if row_of(2 * pair + 1) is not None:
+            put(row_of(2 * pair + 1), seconds)
+
+
+def pack_out(slab, take, sent):
     half = slab.block_x * slab.planes
     first_half = lane_index() < half
-    zero = jnp.zeros((SUBLANES, LANES), F32)
 
     def by_gy(row):
         return swap_groups([take(row, tile) for tile in range(slab.tiles)], slab.deep)
 
-    for pair in range(14):
-        firsts = by_gy(2 * pair)
-        seconds = by_gy(2 * pair + 1) if 2 * pair + 1 < 27 else [zero] * slab.gy
+    for pair in range(MOVING // 2):
+        firsts, seconds = by_gy(2 * pair), by_gy(2 * pair + 1)
         for y in range(slab.gy):
             a, b = firsts[y], seconds[y]
-            flow_out[y, pair] = jnp.where(first_half, a, lane_roll(b, half))
-            flow_out[slab.gy + y, pair] = jnp.where(first_half, lane_roll(a, half), b)
-    fields = [by_gy(HEAT_AT + k) for k in range(7)]
-    for y in range(slab.gy):
-        sources = [fields[k][y] for k in range(7)] + [zero]
-        for number, value in enumerate(swap_groups(sources, slab.planes)):
-            x, part = number // slab.grp, number % slab.grp
-            heat_out[(part * slab.gx + x) * slab.gy + y] = value
-
-
-def unpack_out(slab, flow_ref, heat_ref, popul_out, thermal_out):
-    for pair in range(14):
-        sources = [flow_ref[source, pair] for source in range(slab.sub)]
-        for number, value in enumerate(swap_groups(sources, slab.planes)):
-            field, x = 2 * pair + number // slab.block_x, number % slab.block_x
-            if field < 27:
-                popul_out[field, x] = value
-    for part in range(slab.grp):
-        sources = [heat_ref[part * slab.sub + source] for source in range(slab.sub)]
-        for k, value in enumerate(swap_groups(sources, slab.planes)[:7]):
-            thermal_out[k, 0, :, pl.ds(part * LANES, LANES)] = value
+            sent[y, pair] = jnp.where(first_half, a, lane_roll(b, half))
+            sent[slab.gy + y, pair] = jnp.where(first_half, lane_roll(a, half), b)
+
+
+def unpack_pair(slab, came, pair):
+    mine = lax.axis_index("grp")
+    sources = [came[slab.holder(place, mine), pair] for place in range(slab.sub)]
+    for number, value in enumerate(swap_groups(sources, slab.planes)):
+        yield 2 * pair + number // slab.block_x, number % slab.block_x, value
+
+
+def return_heat(slab, came, *refs):
+    outs, held = refs[: slab.grp], refs[slab.grp]
+    for pair in range(HEAT_AT // 2, MOVING // 2):
+        for row, x, value in unpack_pair(slab, came, pair):
+            if row >= HEAT_AT:
+                held[x, row - HEAT_AT] = value
+    mine = lax.axis_index("grp")
+    for step in range(slab.grp):
+        outs[step][...] = held[jnp.bitwise_xor(mine, step)]
+
+
+def unpack_flow(slab, came, popul_out):
+    for pair in range((HEAT_AT + 1) // 2):
+        for row, x, value in unpack_pair(slab, came, pair):
+            if row < HEAT_AT:
+                popul_out[row, x] = value
+
+
+def join_heat(slab, *refs):
+    parts, thermal_out = refs[: slab.grp], refs[slab.grp]
+    mine = lax.axis_index("grp")
+    for step in range(slab.grp):
+        part = jnp.bitwise_xor(mine, step)
+        span = pl.ds(pl.multiple_of(part * LANES, LANES), LANES)
+        for k in range(7):
+            thermal_out[k, 0, :, span] = parts[step][k]
 
 
 def forward3(values):
@@ -546,7 +625,16 @@
     return BUOYANCY * (total - REFERENCE_HEAT)
 
 
-def first_window(slab, rates_ref, own_ref, low_ref, high_ref, own_out, low_out, high_out, keep_out, state, post, speed):
+def fetch(source, target, sem):
+    copy = pltpu.make_async_copy(source, target, sem)
+    copy.start()
+    copy.wait()
+
+
+def first_window(slab, rates_hbm, own_ref, low_ref, high_ref, *refs):
+    own_out, low_out, high_out, keep_out, rates_ref, sem, state, post, speed = refs
+    fetch(rates_hbm, rates_ref, sem)
+
     def gather(row, tile):
         if tile == 0:
             return low_ref[row]
@@ -600,70 +688,103 @@
         force[tile] = heat_force(state, tile)
 
 
-def last_window(slab, rates_ref, own_ref, low_ref, high_ref, keep_ref, flow_out, heat_out, state, post, speed, force):
+def last_window(slab, rates_hbm, own_ref, low_ref, high_ref, keep_ref, *refs):
+    sent, rates_ref, sem, state, post, speed, force = refs
+    fetch(rates_hbm, rates_ref, sem)
     next_state(slab, own_ref, low_ref, high_ref, keep_ref, state, speed, force)
     run_steps(slab, rates_ref, state, post, force, keep_ref.at[0], speed, keep_ref.at[1])
-    pack_out(slab, lambda row, tile: state[row, tile + 1], flow_out, heat_out)
-
-
-def middle_window(slab, rates_ref, own_ref, low_ref, high_ref, keep_ref, own_out, low_out, high_out, keep_out, state, post, speed):
-    for k in range(2):
-        for tile in range(slab.padded):
-            keep_out[k, tile] = keep_ref[k, tile]
-    next_state(slab, own_ref, low_ref, high_ref, keep_ref, state, speed, keep_out.at[2])
-    run_steps(slab, rates_ref, state, post, keep_out.at[2], keep_out.at[0], speed, keep_out.at[1])
-    for row in range(MOVING):
-        for tile in range(slab.tiles):
-            own_out[row, tile] = state[row, tile + 1]
-        low_out[row] = state[row, 1]
-        high_out[row] = state[row, slab.tiles]
-
-
-def local_call(body, slab, scalars, arrays, outs, scratch=()):
+    pack_out(slab, lambda row, tile: state[row, tile + 1], sent)
+
+
+def local_call(body, slab, arrays, outs, scratch=(), in_hbm=0, carried=False):
     def kernel(*refs):
         body(slab, *refs)
 
     return pl.pallas_call(
         kernel,
         out_shape=[jax.ShapeDtypeStruct(shape, F32) for shape in outs],
-        in_specs=[pl.BlockSpec(memory_space=pltpu.SMEM)] * len(scalars)
-        + [pl.BlockSpec(memory_space=pltpu.VMEM)] * len(arrays),
-        out_specs=[pl.BlockSpec(memory_space=pltpu.VMEM)] * len(outs),
-        scratch_shapes=[pltpu.VMEM(shape, F32) for shape in scratch],
+        in_specs=[
+            pl.BlockSpec(
+                memory_space=pltpu.HBM if i < in_hbm else pl.ANY if carried and i == 0 else pltpu.VMEM
+            )
+            for i in range(len(arrays))
+        ],
+        out_specs=[pl.BlockSpec(memory_space=pl.ANY if carried else pltpu.VMEM)] * len(outs),
+        input_output_aliases={0: 0} if carried else {},
+        scratch_shapes=[pltpu.VMEM(s, F32) if isinstance(s, tuple) else s for s in scratch],
         compiler_params=pltpu.CompilerParams(vmem_limit_bytes=24 * 1024 * 1024),
-    )(*scalars, *arrays)
+    )(*(pltpu.with_memory_space_constraint(a, pltpu.HBM) if i < in_hbm else a for i, a in enumerate(arrays)))
 
 
 RING = ("grp", "gx", "gy")
 
 
-def exchange(low, high, count):
-    from_below = lax.ppermute(high, RING, [(i, (i + 1) % count) for i in range(count)])
-    from_above = lax.ppermute(low, RING, [((i + 1) % count, i) for i in range(count)])
+def exchange(slab, low, high):
+    ring = slab.ring
+    upward = [(ring[i - 1], ring[i]) for i in range(len(ring))]
+    from_below = lax.ppermute(high, RING, upward)
+    from_above = lax.ppermute(low, RING, [(b, a) for a, b in upward])
     return from_below, from_above
+
+
+def across_planes(slab, parts):
+    return [parts[0]] + [
+        lax.ppermute(parts[step], "grp", [(i, i ^ step) for i in range(slab.grp)])
+        for step in range(1, slab.grp)
+    ]
 
 
 def on_slabs(slab, populations, thermal, velocity_prev, solid, phase_ids, conductivity, rates):
     tile = (SUBLANES, LANES)
-    count = slab.grp * slab.sub
-
-    def pack_body(slab, levels_ref, popul_ref, speed_ref, solid_ref, heat_ref, phase_ref, flow_out, heat_out):
-        pack_in(slab, popul_ref, speed_ref, solid_ref, heat_ref, phase_ref, levels_ref, flow_out, heat_out)
-
-    flow, heat = local_call(
-        pack_body,
+
+    def vmem_like(array):
+        return pltpu.VMEM(array.shape, array.dtype)
+
+    parts = local_call(
+        offer_heat,
         slab,
-        [conductivity],
-        [populations, velocity_prev, solid, thermal, phase_ids],
-        [(slab.sub, 16) + tile, (count,) + tile],
-    )
-    heat = lax.all_to_all(heat, RING, split_axis=0, concat_axis=0, tiled=True)
-    flow = lax.all_to_all(flow, ("gx", "gy"), split_axis=0, concat_axis=0, tiled=True)
+        [conductivity, thermal, phase_ids],
+        [(8,) + tile] * slab.grp,
+        [
+            pltpu.SMEM(conductivity.shape, F32),
+            vmem_like(thermal),
+            vmem_like(phase_ids),
+            pltpu.SemaphoreType.DMA((3,)),
+        ],
+        in_hbm=3,
+    )
+    parts = across_planes(slab, parts)
+    sent_shape = (slab.sub, SENT // 2) + tile
+    sent, flags = local_call(
+        pack_flow,
+        slab,
+        [populations, velocity_prev, solid],
+        [sent_shape, solid.shape],
+        [
+            vmem_like(populations),
+            vmem_like(velocity_prev),
+            vmem_like(solid),
+            pltpu.SemaphoreType.DMA((4,)),
+        ],
+        in_hbm=3,
+    )
+    (sent,) = local_call(
+        pack_heat,
+        slab,
+        [sent, flags] + parts,
+        [sent_shape],
+        [
+            (slab.grp, 8) + tile,
+            (slab.sub, (SENT - SENT_SOLID) // 2) + tile,
+            pltpu.SemaphoreType.DMA,
+        ],
+        carried=True,
+    )
+    came = lax.all_to_all(sent, ("gx", "gy"), split_axis=0, concat_axis=0, tiled=True)
     own, low, high = local_call(
         unpack_in,
         slab,
-        [],
-        [flow, heat],
+        [came],
         [(ROWS, slab.tiles) + tile, (ROWS,) + tile, (ROWS,) + tile],
     )
     window_outs = [
@@ -672,41 +793,34 @@
         (MOVING,) + tile,
         (3, slab.padded) + tile,
     ]
-    lattice = (MOVING, slab.padded) + tile
-    below, above = exchange(low, high, count)
+    window_scratch = [
+        pltpu.SMEM(rates.shape, F32),
+        pltpu.SemaphoreType.DMA,
+        (MOVING, slab.padded) + tile,
+        (MOVING, slab.padded) + tile,
+        (3, slab.padded) + tile,
+    ]
+    below, above = exchange(slab, low, high)
     own, low, high, keep = local_call(
-        first_window,
+        first_window, slab, [rates, own, below, above], window_outs, window_scratch, in_hbm=1
+    )
+    below, above = exchange(slab, low, high)
+    (sent,) = local_call(
+        last_window,
         slab,
-        [rates],
-        [own, below, above],
-        window_outs,
-        [lattice, lattice, (3, slab.padded) + tile],
-    )
-    for number in range(1, WINDOWS):
-        below, above = exchange(low, high, count)
-        if number + 1 < WINDOWS:
-            own, low, high, keep = local_call(
-                middle_window,
-                slab,
-                [rates],
-                [own, below, above, keep],
-                window_outs,
-                [lattice, lattice, (3, slab.padded) + tile],
-            )
-        else:
-            flow, heat = local_call(
-                last_window,
-                slab,
-                [rates],
-                [own, below, above, keep],
-                [(slab.sub, 14) + tile, (count,) + tile],
-                [lattice, lattice, (3, slab.padded) + tile, (slab.padded,) + tile],
-            )
-    flow = lax.all_to_all(flow, ("gx", "gy"), split_axis=0, concat_axis=0, tiled=True)
-    heat = lax.all_to_all(heat, RING, split_axis=0, concat_axis=0, tiled=True)
-    return tuple(
-        local_call(unpack_out, slab, [], [flow, heat], [populations.shape, thermal.shape])
-    )
+        [rates, own, below, above, keep],
+        [(slab.sub, MOVING // 2) + tile],
+        window_scratch + [(slab.padded,) + tile],
+        in_hbm=1,
+    )
+    came = lax.all_to_all(sent, ("gx", "gy"), split_axis=0, concat_axis=0, tiled=True)
+    parts = local_call(
+        return_heat, slab, [came], [(7,) + tile] * slab.grp, [(slab.grp, 7) + tile]
+    )
+    parts = across_planes(slab, parts)
+    (populations_out,) = local_call(unpack_flow, slab, [came], [populations.shape])
+    (thermal_out,) = local_call(join_heat, slab, parts, [thermal.shape])
+    return populations_out, thermal_out
 
 
 def solution(mesh):
@@ -723,7 +837,7 @@
 
     def per_device(populations, thermal, *others):
         slab = Slab(mesh.shape, populations.shape[1:], thermal.shape[1:])
-        plan = (lambda *arrays: on_slabs(slab, *arrays)) if slab.fits and WINDOWS > 1 else on_device
+        plan = (lambda *arrays: on_slabs(slab, *arrays)) if slab.fits and WINDOWS == 2 else on_device
         return plan(populations, thermal, *others)
 
     return jax.shard_map(

time: 103 us -> 88.5 us (0.86)
  blocking collectives: 52.7 us -> 27.1 us
  waiting for transfers between devices: 5.63 us -> 13.9 us
  starting transfers between devices: 10.8 us -> 18 us
  local copies, waits for them, and re-layouts: 4.8 us -> 0 us
    all_to_all x4 -> x2, blocking collectives: 52.7 us -> 27.1 us  [on_slabs(): lax.all_to_all(sent, ('gx', 'gy'), split_axis=0, concat_axis=0, tiled=True)]
    ppermute x4 -> x10, waiting for transfers between devices: 5.63 us -> 13.9 us  [the longest x6 7.73 us: across_planes(): lax.ppermute(parts[step], 'grp', [(i, i ^ step) for i in range(slab.grp)])]
    ppermute x4 -> x10, starting transfers between devices: 10.8 us -> 18 us  [the longest x6 10.2 us: across_planes(): lax.ppermute(parts[step], 'grp', [(i, i ^ step) for i in range(slab.grp)])]
    unnamed x14 -> x0, local copies, waits for them, and re-layouts: 4.8 us -> none
    pallas_call x5 -> x9, Pallas kernels: 27.8 us -> 28.4 us  [local_call(): pl.pallas_call(kernel, out_shape=[jax.ShapeDtypeStruct(shape, F32) for sh...]
  transfers between devices with their start and end apart: 4 -> 10, of which waited for: 2 -> 6; matrix products, arithmetic and copies ran while one was open for 0% -> 0% of each run, Pallas kernels for 0% -> 4%
where the time goes in v1:
time: 88.5 us; the launch traced here: 88.3 us
  Pallas kernels  28.4 us (32%)
  blocking collectives  27.1 us (31%)
  starting transfers between devices  18 us (20%)
  waiting for transfers between devices  13.9 us (16%)
    pallas_call x9, Pallas kernels, local_call(): pl.pallas_call(kernel, out_shape=[jax.ShapeDtypeStruct(shape, F32) for sh...  28.4 us
    all_to_all x2, blocking collectives, on_slabs(): lax.all_to_all(sent, ('gx', 'gy'), split_axis=0, concat_axis=0, tiled=True)  27.1 us
    ppermute x6, starting transfers between devices, across_planes(): lax.ppermute(parts[step], 'grp', [(i, i ^ step) for i in range(slab.grp)])  10.2 us
    ppermute x6, waiting for transfers between devices, across_planes(): lax.ppermute(parts[step], 'grp', [(i, i ^ step) for i in range(slab.grp)])  7.73 us
    ppermute x2, starting transfers between devices, exchange(): from_above = lax.ppermute(low, RING, [(b, a) for a, b in upward])  7.69 us
    ppermute x2, waiting for transfers between devices, exchange(): from_below = lax.ppermute(high, RING, upward)  6.21 us
  transfers between devices with their start and end apart: 10, of which 6 were waited for; matrix products, arithmetic and copies ran while one was open for 0% of the time, Pallas kernels for 4%

profile of v1, /device:TPU:0, one launch (start us, length us, event | category | flops | bytes accessed | tf_op | source)
XLA Modules:
  0.0 88.3 jit_solution(5126326619633913292)
XLA Ops:
  0.6 1.0 %shard_map.87 = (f32[8,8,128]{2,1,0:T(8,128)S(1)}, f32[8,8,128]{2,1,0:T(8,128)S(1)}, f32[8,8,128]{2,1,0:T(8,128)S(1)}, f32[8,8,128]{2,1,0:T(8,128)S(1)}) custom-call(f32[4]{0:T(128)} %refs_0_.5, f32[7,1,8,512]{3,2,1,0:T(8,128)} %refs_1_.3, s32[1,8,512]{2,1,0:T(8,128)} %refs_2_.3), custom_call_target="tpu_custom_call" | custom-call | tf_op jit(solution)/shard_map/pallas_call | solution.py:703
  1.6 3.1 %collective-permute-start = (f32[8,8,128]{2,1,0:T(8,128)S(1)}, f32[8,8,128]{2,1,0:T(8,128)S(1)}, u32[]{:S(2)}, u32[]{:S(2)}) collective-permute-start(f32[8,8,128]{2,1,0:T(8,128)S(1)} %get-tuple-element.22), channel_id=1, source_target_pairs={{0,8},{8,0},{16,24},{24,16},{1,9},{9,1},{17,25},{25,17},{2,10},{10... | collective-permute-start | bytes 98312 | tf_op jit(solution)/shard_map/ppermute | solution.py:732
  4.7 2.6 %collective-permute-start.1 = (f32[8,8,128]{2,1,0:T(8,128)S(1)}, f32[8,8,128]{2,1,0:T(8,128)S(1)}, u32[]{:S(2)}, u32[]{:S(2)}) collective-permute-start(f32[8,8,128]{2,1,0:T(8,128)S(1)} %get-tuple-element.23), channel_id=1, source_target_pairs={{0,16},{8,24},{16,0},{24,8},{1,17},{9,25},{17,1},{25,9},{2,18},{10... | collective-permute-start | bytes 98312 | tf_op jit(solution)/shard_map/ppermute | solution.py:732
  7.3 0.0 collective-permute-start.2
  7.3 1.8 %shard_map.86 = (f32[8,20,8,128]{3,2,1,0:T(8,128)S(1)}, f32[4,8,128]{2,1,0:T(8,128)S(1)}) custom-call(f32[27,4,8,128]{3,2,1,0:T(8,128)} %refs_0_.4, f32[3,4,8,128]{3,2,1,0:T(8,128)} %refs_1_.2, s32[4,8,128]{2,1,0:T(8,128)} %refs_2_.2), custom_call_target="tpu_custom_call" | custom-call | tf_op jit(solution)/shard_map/pallas_call | solution.py:703
  9.1 0.0 collective-permute-done.refs_3_
  9.1 1.0 %collective-permute-done.1.refs_4_ = f32[8,8,128]{2,1,0:T(8,128)S(1)} collective-permute-done((f32[8,8,128]{2,1,0:T(8,128)S(1)}, f32[8,8,128]{2,1,0:T(8,128)S(1)}, u32[]{:S(2)}, u32[]{:S(2)}) %collective-permute-start.1) | collective-permute-done | bytes 32800 | tf_op jit(solution)/shard_map/ppermute | solution.py:732
  10.1 2.9 %collective-permute-done.2.refs_5_ = f32[8,8,128]{2,1,0:T(8,128)S(1)} collective-permute-done((f32[8,8,128]{2,1,0:T(8,128)S(1)}, f32[8,8,128]{2,1,0:T(8,128)S(1)}, u32[]{:S(2)}, u32[]{:S(2)}) %collective-permute-start.2) | collective-permute-done | bytes 32800 | tf_op jit(solution)/shard_map/ppermute | solution.py:732
  13.0 0.3 shard_map.88
  13.3 14.7 %all_to_all.10.refs_0_ = f32[8,20,8,128]{3,2,1,0:T(8,128)S(1)} all-to-all(f32[8,20,8,128]{3,2,1,0:T(8,128)S(1)} %shard_map.88), channel_id=1, replica_groups=mesh['grp'=4,'gx'=2,'gy'=4] {'gx','gy'}, dimensions={0} | all-to-all | bytes 1310720 | tf_op jit(solution)/shard_map/all_to_all | solution.py:783
  28.0 2.7 %shard_map.89 = (f32[39,4,8,128]{3,2,1,0:T(8,128)S(1)}, f32[39,8,128]{2,1,0:T(8,128)S(1)}, f32[39,8,128]{2,1,0:T(8,128)S(1)}) custom-call(f32[8,20,8,128]{3,2,1,0:T(8,128)S(1)} %all_to_all.10.refs_0_), custom_call_target="tpu_custom_call" | custom-call | tf_op jit(solution)/shard_map/pallas_call | solution.py:703
  30.7 0.1 collective-permute-start.3
  30.8 3.8 %collective-permute-start.4 = (f32[39,8,128]{2,1,0:T(8,128)S(1)}, f32[39,8,128]{2,1,0:T(8,128)S(1)}, u32[]{:S(2)}, u32[]{:S(2)}) collective-permute-start(f32[39,8,128]{2,1,0:T(8,128)S(1)} %get-tuple-element.27), channel_id=1, source_target_pairs={{0,24},{1,0},{2,1},{3,2},{7,3},{6,7},{5,6},{4,5},{12,4},{13,12},{1... | collective-permute-start | bytes 479240 | tf_op jit(solution)/shard_map/ppermute | solution.py:726
  34.6 3.2 %collective-permute-done.3.refs_2_ = f32[39,8,128]{2,1,0:T(8,128)S(1)} collective-permute-done((f32[39,8,128]{2,1,0:T(8,128)S(1)}, f32[39,8,128]{2,1,0:T(8,128)S(1)}, u32[]{:S(2)}, u32[]{:S(2)}) %collective-permute-start.3) | collective-permute-done | bytes 159776 | tf_op jit(solution)/shard_map/ppermute | solution.py:725
  37.9 0.0 collective-permute-done.4.refs_3_
  37.9 8.8 %shard_map.90 = (f32[34,4,8,128]{3,2,1,0:T(8,128)S(1)}, f32[34,8,128]{2,1,0:T(8,128)S(1)}, f32[34,8,128]{2,1,0:T(8,128)S(1)}, f32[3,6,8,128]{3,2,1,0:T(8,128)S(1)}) custom-call(f32[27]{0:T(128)} %refs_0_.7, f32[39,4,8,128]{3,2,1,0:T(8,128)S(1)} %get-tuple-element.25.refs_1_, f32[39,8,128]{2,1,0:T(8,128)S(1)} %collective-permute-done.3.refs_2_, ...), custom_call_target="tpu_custom_call" | custom-call | tf_op jit(solution)/shard_map/pallas_call | solution.py:703
  46.7 0.1 collective-permute-start.5
  46.7 3.9 %collective-permute-start.6 = (f32[34,8,128]{2,1,0:T(8,128)S(1)}, f32[34,8,128]{2,1,0:T(8,128)S(1)}, u32[]{:S(2)}, u32[]{:S(2)}) collective-permute-start(f32[34,8,128]{2,1,0:T(8,128)S(1)} %get-tuple-element.30), channel_id=1, source_target_pairs={{0,24},{1,0},{2,1},{3,2},{7,3},{6,7},{5,6},{4,5},{12,4},{13,12},{1... | collective-permute-start | bytes 417800 | tf_op jit(solution)/shard_map/ppermute | solution.py:726
  50.6 3.0 %collective-permute-done.5.refs_2_ = f32[34,8,128]{2,1,0:T(8,128)S(1)} collective-permute-done((f32[34,8,128]{2,1,0:T(8,128)S(1)}, f32[34,8,128]{2,1,0:T(8,128)S(1)}, u32[]{:S(2)}, u32[]{:S(2)}) %collective-permute-start.5) | collective-permute-done | bytes 139296 | tf_op jit(solution)/shard_map/ppermute | solution.py:725
  53.6 0.0 collective-permute-done.6.refs_3_
  53.6 11.1 %shard_map.91 = f32[8,17,8,128]{3,2,1,0:T(8,128)S(1)} custom-call(f32[27]{0:T(128)} %refs_0_.7, f32[34,4,8,128]{3,2,1,0:T(8,128)S(1)} %get-tuple-element.28.refs_1_, f32[34,8,128]{2,1,0:T(8,128)S(1)} %collective-permute-done.5.refs_2_, f32[34,8,128]{2,1,0:T(8,128)S(1)} %collective-permute-done.6.refs_3_, f32[3,6,8,128]{3,2,1,0:T(8,128)S(1)} %get-tuple-element.31.refs_4_), custom_call_target="tpu_custom_call" | custom-call | tf_op jit(solution)/shard_map/pallas_call | solution.py:703
  64.7 12.5 %all_to_all.11.refs_0_ = f32[8,17,8,128]{3,2,1,0:T(8,128)S(1)} all-to-all(f32[8,17,8,128]{3,2,1,0:T(8,128)S(1)} %shard_map.91), channel_id=1, replica_groups=mesh['grp'=4,'gx'=2,'gy'=4] {'gx','gy'}, dimensions={0} | all-to-all | bytes 1114112 | tf_op jit(solution)/shard_map/all_to_all | solution.py:816
  77.2 0.3 shard_map.93
  77.4 0.1 collective-permute-start.7
  77.5 4.4 %collective-permute-start.8 = (f32[7,8,128]{2,1,0:T(8,128)S(1)}, f32[7,8,128]{2,1,0:T(8,128)S(1)}, u32[]{:S(2)}, u32[]{:S(2)}) collective-permute-start(f32[7,8,128]{2,1,0:T(8,128)S(1)} %get-tuple-element.34), channel_id=1, source_target_pairs={{0,16},{8,24},{16,0},{24,8},{1,17},{9,25},{17,1},{25,9},{2,18},{10... | collective-permute-start | bytes 86024 | tf_op jit(solution)/shard_map/ppermute | solution.py:732
  82.0 0.0 collective-permute-start.9
  82.0 1.9 %shard_map.92 = f32[27,4,8,128]{3,2,1,0:T(8,128)} custom-call(f32[8,17,8,128]{3,2,1,0:T(8,128)S(1)} %all_to_all.11.refs_0_), custom_call_target="tpu_custom_call" | custom-call | tf_op jit(solution)/shard_map/pallas_call | solution.py:703
  83.8 0.0 collective-permute-done.7.refs_1_
  83.8 0.5 collective-permute-done.8.refs_2_
  84.3 3.3 %collective-permute-done.9.refs_3_ = f32[7,8,128]{2,1,0:T(8,128)S(1)} collective-permute-done((f32[7,8,128]{2,1,0:T(8,128)S(1)}, f32[7,8,128]{2,1,0:T(8,128)S(1)}, u32[]{:S(2)}, u32[]{:S(2)}) %collective-permute-start.9) | collective-permute-done | bytes 28704 | tf_op jit(solution)/shard_map/ppermute | solution.py:732
  87.6 0.7 shard_map.94
Async XLA Ops:
  1.6 7.5 %collective-permute-start = (f32[8,8,128]{2,1,0:T(8,128)S(1)}, f32[8,8,128]{2,1,0:T(8,128)S(1)}, u32[]{:S(2)}, u32[]{:S(2)}) collective-permute-start(f32[8,8,128]{2,1,0:T(8,128)S(1)} %get-tuple-element.22), channel_id=1, source_target_pairs={{0,8},{8,0},{16,24},{24,16},{1,9},{9,1},{17,25},{25,17},{2,10},{10... | collective-permute-start | bytes 98312 | tf_op jit(solution)/shard_map/ppermute | solution.py:732
  4.7 5.4 %collective-permute-start.1 = (f32[8,8,128]{2,1,0:T(8,128)S(1)}, f32[8,8,128]{2,1,0:T(8,128)S(1)}, u32[]{:S(2)}, u32[]{:S(2)}) collective-permute-start(f32[8,8,128]{2,1,0:T(8,128)S(1)} %get-tuple-element.23), channel_id=1, source_target_pairs={{0,16},{8,24},{16,0},{24,8},{1,17},{9,25},{17,1},{25,9},{2,18},{10... | collective-permute-start | bytes 98312 | tf_op jit(solution)/shard_map/ppermute | solution.py:732
  7.3 5.7 %collective-permute-start.2 = (f32[8,8,128]{2,1,0:T(8,128)S(1)}, f32[8,8,128]{2,1,0:T(8,128)S(1)}, u32[]{:S(2)}, u32[]{:S(2)}) collective-permute-start(f32[8,8,128]{2,1,0:T(8,128)S(1)} %get-tuple-element.24), channel_id=1, source_target_pairs={{0,24},{8,16},{16,8},{24,0},{1,25},{9,17},{17,9},{25,1},{2,26},{10... | collective-permute-start | bytes 98312 | tf_op jit(solution)/shard_map/ppermute | solution.py:732
  30.7 7.1 %collective-permute-start.3 = (f32[39,8,128]{2,1,0:T(8,128)S(1)}, f32[39,8,128]{2,1,0:T(8,128)S(1)}, u32[]{:S(2)}, u32[]{:S(2)}) collective-permute-start(f32[39,8,128]{2,1,0:T(8,128)S(1)} %get-tuple-element.26), channel_id=1, source_target_pairs={{24,0},{0,1},{1,2},{2,3},{3,7},{7,6},{6,5},{5,4},{4,12},{12,13},{1... | collective-permute-start | bytes 479240 | tf_op jit(solution)/shard_map/ppermute | solution.py:725
  30.8 7.1 %collective-permute-start.4 = (f32[39,8,128]{2,1,0:T(8,128)S(1)}, f32[39,8,128]{2,1,0:T(8,128)S(1)}, u32[]{:S(2)}, u32[]{:S(2)}) collective-permute-start(f32[39,8,128]{2,1,0:T(8,128)S(1)} %get-tuple-element.27), channel_id=1, source_target_pairs={{0,24},{1,0},{2,1},{3,2},{7,3},{6,7},{5,6},{4,5},{12,4},{13,12},{1... | collective-permute-start | bytes 479240 | tf_op jit(solution)/shard_map/ppermute | solution.py:726
  46.7 6.9 %collective-permute-start.5 = (f32[34,8,128]{2,1,0:T(8,128)S(1)}, f32[34,8,128]{2,1,0:T(8,128)S(1)}, u32[]{:S(2)}, u32[]{:S(2)}) collective-permute-start(f32[34,8,128]{2,1,0:T(8,128)S(1)} %get-tuple-element.29), channel_id=1, source_target_pairs={{24,0},{0,1},{1,2},{2,3},{3,7},{7,6},{6,5},{5,4},{4,12},{12,13},{1... | collective-permute-start | bytes 417800 | tf_op jit(solution)/shard_map/ppermute | solution.py:725
  46.7 6.8 %collective-permute-start.6 = (f32[34,8,128]{2,1,0:T(8,128)S(1)}, f32[34,8,128]{2,1,0:T(8,128)S(1)}, u32[]{:S(2)}, u32[]{:S(2)}) collective-permute-start(f32[34,8,128]{2,1,0:T(8,128)S(1)} %get-tuple-element.30), channel_id=1, source_target_pairs={{0,24},{1,0},{2,1},{3,2},{7,3},{6,7},{5,6},{4,5},{12,4},{13,12},{1... | collective-permute-start | bytes 417800 | tf_op jit(solution)/shard_map/ppermute | solution.py:726
  77.4 6.4 %collective-permute-start.7 = (f32[7,8,128]{2,1,0:T(8,128)S(1)}, f32[7,8,128]{2,1,0:T(8,128)S(1)}, u32[]{:S(2)}, u32[]{:S(2)}) collective-permute-start(f32[7,8,128]{2,1,0:T(8,128)S(1)} %get-tuple-element.33), channel_id=1, source_target_pairs={{0,8},{8,0},{16,24},{24,16},{1,9},{9,1},{17,25},{25,17},{2,10},{10... | collective-permute-start | bytes 86024 | tf_op jit(solution)/shard_map/ppermute | solution.py:732
  77.5 6.8 %collective-permute-start.8 = (f32[7,8,128]{2,1,0:T(8,128)S(1)}, f32[7,8,128]{2,1,0:T(8,128)S(1)}, u32[]{:S(2)}, u32[]{:S(2)}) collective-permute-start(f32[7,8,128]{2,1,0:T(8,128)S(1)} %get-tuple-element.34), channel_id=1, source_target_pairs={{0,16},{8,24},{16,0},{24,8},{1,17},{9,25},{17,1},{25,9},{2,18},{10... | collective-permute-start | bytes 86024 | tf_op jit(solution)/shard_map/ppermute | solution.py:732
  82.0 5.7 %collective-permute-start.9 = (f32[7,8,128]{2,1,0:T(8,128)S(1)}, f32[7,8,128]{2,1,0:T(8,128)S(1)}, u32[]{:S(2)}, u32[]{:S(2)}) collective-permute-start(f32[7,8,128]{2,1,0:T(8,128)S(1)} %get-tuple-element.35), channel_id=1, source_target_pairs={{0,24},{8,16},{16,8},{24,0},{1,25},{9,17},{17,9},{25,1},{2,26},{10... | collective-permute-start | bytes 86024 | tf_op jit(solution)/shard_map/ppermute | solution.py:732

commit v2 on v1

--- a/solution.py
+++ b/solution.py
@@ -239,10 +239,12 @@
             and self.sub & (self.sub - 1) == 0
             and self.gy & (self.gy - 1) == 0
             and self.grp & (self.grp - 1) == 0
+            and self.planes >= self.deep * WINDOWS
         )
         if self.fits:
             self.tiles = self.planes // self.deep
-            self.padded = self.tiles + 2
+            self.margin = WINDOWS
+            self.padded = self.tiles + 2 * self.margin
             self.snake = [
                 x * self.gy + (y if x % 2 == 0 else self.gy - 1 - y)
                 for x in range(self.gx)
@@ -392,10 +394,10 @@
     def put(row, by_gy):
         for tile, value in enumerate(swap_groups(by_gy, slab.deep)):
             state_out[row, tile] = value
-            if tile == 0:
-                low_out[row] = value
-            if tile == slab.tiles - 1:
-                high_out[row] = value
+            if tile < slab.margin:
+                low_out[row, tile] = value
+            if tile >= slab.tiles - slab.margin:
+                high_out[row, tile - (slab.tiles - slab.margin)] = value
 
     for pair in range(SENT // 2):
         firsts, seconds = [], []
@@ -562,10 +564,8 @@
 HEAT_OFFSETS = [(0, 0, 0), (1, 0, 0), (-1, 0, 0), (0, 1, 0), (0, -1, 0), (0, 0, 1), (0, 0, -1)]
 
 
-def run_steps(slab, rates_ref, state, post, force_ref, rate_ref, speed_ref, solid_ref):
-    last = slab.padded - 1
-
-    def collide_one(tile, _):
+def run_steps(slab, rates_ref, state, post, force_ref, rate_ref, speed_ref, solid_ref, tiles):
+    def collide_one(tile):
         values = [state[n, tile] for n in range(27)]
         solid = solid_ref[tile] != 0.0
         moved = collide_tile(values, force_ref[tile], lambda n: rates_ref[n])
@@ -577,19 +577,18 @@
             total = total + heat[k]
         omega = rate_ref[tile]
         side = 0.125 * total
+        half = 0.5 * total
         for k in range(7):
             if k == 0:
                 level = 0.25 * total
             else:
-                drift = (0.5 * total) * speed_ref[(k - 1) // 2, tile]
+                drift = half * speed_ref[(k - 1) // 2, tile]
                 level = side + drift if k % 2 == 1 else side - drift
             post[HEAT_AT + k, tile] = heat[k] - (heat[k] - level) * omega
-        return 0
-
-    def stream_one(tile, _):
-        along_x, along_y, along_z = shifters(slab)
-        before = jnp.where(tile == 0, last, tile - 1)
-        after = jnp.where(tile == last, 0, tile + 1)
+
+    def stream_one(tile, shifts):
+        along_x, along_y, along_z = shifts
+        before, after = max(tile - 1, tiles[0]), min(tile + 1, tiles[-1])
         solid = solid_ref[tile] != 0.0
 
         def arrive(row, offset):
@@ -608,11 +607,14 @@
             state[n, tile] = jnp.where(solid, state[n, tile], value)
         for k in range(7):
             state[HEAT_AT + k, tile] = arrive(HEAT_AT + k, HEAT_OFFSETS[k])
-        return 0
 
     def step(number, _):
-        lax.fori_loop(0, slab.padded, collide_one, 0)
-        lax.fori_loop(0, slab.padded, stream_one, 0)
+        shifts = shifters(slab)
+        for tile in tiles:
+            collide_one(tile)
+            if tile > tiles[0]:
+                stream_one(tile - 1, shifts)
+        stream_one(tiles[-1], shifts)
         return 0
 
     lax.fori_loop(0, STEPS, step, 0)
@@ -625,75 +627,57 @@
     return BUOYANCY * (total - REFERENCE_HEAT)
 
 
-def fetch(source, target, sem):
-    copy = pltpu.make_async_copy(source, target, sem)
-    copy.start()
-    copy.wait()
-
-
-def first_window(slab, rates_hbm, own_ref, low_ref, high_ref, *refs):
-    own_out, low_out, high_out, keep_out, rates_ref, sem, state, post, speed = refs
-    fetch(rates_hbm, rates_ref, sem)
+def flow_speed_tile(state, tile, force):
+    values = [state[n, tile] for n in range(27)]
+    total = values[0]
+    for n in range(1, 27):
+        total = total + values[n]
+    sums = []
+    for d in range(3):
+        plus, minus = None, None
+        for n in range(27):
+            part = OFFSET_TABLE[n][d]
+            if part == 1:
+                plus = values[n] if plus is None else plus + values[n]
+            if part == -1:
+                minus = values[n] if minus is None else minus + values[n]
+        sums.append(plus - minus)
+    sums[2] = sums[2] + 0.5 * force
+    return [each / total for each in sums]
+
+
+def both_windows(slab, rates_hbm, own_ref, low_ref, high_ref, *refs):
+    sent, rates_ref, sem, state, post, speed, force, rate_ref, solid_ref = refs
+    rates_copy = pltpu.make_async_copy(rates_hbm, rates_ref, sem)
+    rates_copy.start()
+    margin = slab.margin
 
     def gather(row, tile):
-        if tile == 0:
-            return low_ref[row]
-        if tile == slab.padded - 1:
-            return high_ref[row]
-        return own_ref[row, tile - 1]
+        if tile < margin:
+            return low_ref[row, tile]
+        if tile >= slab.padded - margin:
+            return high_ref[row, tile - (slab.padded - margin)]
+        return own_ref[row, tile - margin]
 
     for tile in range(slab.padded):
         for row in range(MOVING):
             state[row, tile] = gather(row, tile)
         for d in range(3):
             speed[d, tile] = gather(SPEED_AT + d, tile)
-        keep_out[0, tile] = gather(RATE_AT, tile)
-        keep_out[1, tile] = gather(SOLID_AT, tile)
-        keep_out[2, tile] = heat_force(state, tile)
-    run_steps(slab, rates_ref, state, post, keep_out.at[2], keep_out.at[0], speed, keep_out.at[1])
-    for row in range(MOVING):
-        for tile in range(slab.tiles):
-            own_out[row, tile] = state[row, tile + 1]
-        low_out[row] = state[row, 1]
-        high_out[row] = state[row, slab.tiles]
-
-
-def next_state(slab, own_ref, low_ref, high_ref, keep_ref, state, speed, force):
-    for tile in range(slab.padded):
-        for row in range(MOVING):
-            if tile == 0:
-                state[row, tile] = low_ref[row]
-            elif tile == slab.padded - 1:
-                state[row, tile] = high_ref[row]
-            else:
-                state[row, tile] = own_ref[row, tile - 1]
-        values = [state[n, tile] for n in range(27)]
-        total = values[0]
-        for n in range(1, 27):
-            total = total + values[n]
-        sums = []
-        for d in range(3):
-            plus, minus = None, None
-            for n in range(27):
-                part = OFFSET_TABLE[n][d]
-                if part == 1:
-                    plus = values[n] if plus is None else plus + values[n]
-                if part == -1:
-                    minus = values[n] if minus is None else minus + values[n]
-            sums.append(plus - minus)
-        sums[2] = sums[2] + 0.5 * keep_ref[2, tile]
-        solid = keep_ref[1, tile] != 0.0
-        for d in range(3):
-            speed[d, tile] = jnp.where(solid, 0.0, sums[d] / total)
+        rate_ref[tile] = gather(RATE_AT, tile)
+        solid_ref[tile] = gather(SOLID_AT, tile)
         force[tile] = heat_force(state, tile)
-
-
-def last_window(slab, rates_hbm, own_ref, low_ref, high_ref, keep_ref, *refs):
-    sent, rates_ref, sem, state, post, speed, force = refs
-    fetch(rates_hbm, rates_ref, sem)
-    next_state(slab, own_ref, low_ref, high_ref, keep_ref, state, speed, force)
-    run_steps(slab, rates_ref, state, post, force, keep_ref.at[0], speed, keep_ref.at[1])
-    pack_out(slab, lambda row, tile: state[row, tile + 1], sent)
+    rates_copy.wait()
+    for window in range(WINDOWS):
+        tiles = list(range(window, slab.padded - window))
+        if window > 0:
+            for tile in tiles:
+                solid = solid_ref[tile] != 0.0
+                for d, each in enumerate(flow_speed_tile(state, tile, force[tile])):
+                    speed[d, tile] = jnp.where(solid, 0.0, each)
+                force[tile] = heat_force(state, tile)
+        run_steps(slab, rates_ref, state, post, force, rate_ref, speed, solid_ref, tiles)
+    pack_out(slab, lambda row, tile: state[row, tile + margin], sent)
 
 
 def local_call(body, slab, arrays, outs, scratch=(), in_hbm=0, carried=False):
@@ -713,7 +697,12 @@
         input_output_aliases={0: 0} if carried else {},
         scratch_shapes=[pltpu.VMEM(s, F32) if isinstance(s, tuple) else s for s in scratch],
         compiler_params=pltpu.CompilerParams(vmem_limit_bytes=24 * 1024 * 1024),
-    )(*(pltpu.with_memory_space_constraint(a, pltpu.HBM) if i < in_hbm else a for i, a in enumerate(arrays)))
+    )(
+        *(
+            pltpu.with_memory_space_constraint(array, pltpu.HBM) if i < in_hbm else array
+            for i, array in enumerate(arrays)
+        )
+    )
 
 
 RING = ("grp", "gx", "gy")
@@ -785,32 +774,24 @@
         unpack_in,
         slab,
         [came],
-        [(ROWS, slab.tiles) + tile, (ROWS,) + tile, (ROWS,) + tile],
-    )
-    window_outs = [
-        (MOVING, slab.tiles) + tile,
-        (MOVING,) + tile,
-        (MOVING,) + tile,
-        (3, slab.padded) + tile,
-    ]
-    window_scratch = [
-        pltpu.SMEM(rates.shape, F32),
-        pltpu.SemaphoreType.DMA,
-        (MOVING, slab.padded) + tile,
-        (MOVING, slab.padded) + tile,
-        (3, slab.padded) + tile,
-    ]
-    below, above = exchange(slab, low, high)
-    own, low, high, keep = local_call(
-        first_window, slab, [rates, own, below, above], window_outs, window_scratch, in_hbm=1
+        [(ROWS, slab.tiles) + tile, (ROWS, slab.margin) + tile, (ROWS, slab.margin) + tile],
     )
     below, above = exchange(slab, low, high)
     (sent,) = local_call(
-        last_window,
+        both_windows,
         slab,
-        [rates, own, below, above, keep],
+        [rates, own, below, above],
         [(slab.sub, MOVING // 2) + tile],
-        window_scratch + [(slab.padded,) + tile],
+        [
+            pltpu.SMEM(rates.shape, F32),
+            pltpu.SemaphoreType.DMA,
+            (MOVING, slab.padded) + tile,
+            (MOVING, slab.padded) + tile,
+            (3, slab.padded) + tile,
+            (slab.padded,) + tile,
+            (slab.padded,) + tile,
+            (slab.padded,) + tile,
+        ],
         in_hbm=1,
     )
     came = lax.all_to_all(sent, ("gx", "gy"), split_axis=0, concat_axis=0, tiled=True)
@@ -837,7 +818,7 @@
 
     def per_device(populations, thermal, *others):
         slab = Slab(mesh.shape, populations.shape[1:], thermal.shape[1:])
-        plan = (lambda *arrays: on_slabs(slab, *arrays)) if slab.fits and WINDOWS == 2 else on_device
+        plan = (lambda *arrays: on_slabs(slab, *arrays)) if slab.fits else on_device
         return plan(populations, thermal, *others)
 
     return jax.shard_map(

time: 88.5 us -> 148 us (1.67)
  Pallas kernels: 28.4 us -> 93 us
  starting transfers between devices: 18 us -> 14 us
    pallas_call x9 -> x8, Pallas kernels: 28.4 us -> 93 us  [local_call(): pl.pallas_call(kernel, out_shape=[jax.ShapeDtypeStruct(shape, F32) for sh...]
    ppermute x2 -> x1, starting transfers between devices: 7.69 us -> 3.81 us  [exchange(): from_above = lax.ppermute(low, RING, [(b, a) for a, b in upward])]
    ppermute x2 -> x1, waiting for transfers between devices: 6.21 us -> 5.07 us  [exchange(): from_below = lax.ppermute(high, RING, upward)]
  transfers between devices with their start and end apart: 10 -> 8, of which waited for: 6 -> 5; matrix products, arithmetic and copies ran while one was open for 0% -> 0% of each run, Pallas kernels for 4% -> 2%
where the time goes in v2:
time: 148 us
  Pallas kernels  93 us (63%)
  blocking collectives  27.1 us (18%)
  starting transfers between devices  14 us (9%)
  waiting for transfers between devices  12.7 us (9%)
    pallas_call x8, Pallas kernels, local_call(): pl.pallas_call(kernel, out_shape=[jax.ShapeDtypeStruct(shape, F32) for sh...  93 us
    all_to_all x2, blocking collectives, on_slabs(): lax.all_to_all(sent, ('gx', 'gy'), split_axis=0, concat_axis=0, tiled=True)  27.1 us
    ppermute x6, starting transfers between devices, across_planes(): lax.ppermute(parts[step], 'grp', [(i, i ^ step) for i in range(slab.grp)])  10.1 us
    ppermute x6, waiting for transfers between devices, across_planes(): lax.ppermute(parts[step], 'grp', [(i, i ^ step) for i in range(slab.grp)])  7.62 us
    ppermute x1, waiting for transfers between devices, exchange(): from_below = lax.ppermute(high, RING, upward)  5.07 us
    ppermute x1, starting transfers between devices, exchange(): from_above = lax.ppermute(low, RING, [(b, a) for a, b in upward])  3.81 us
  transfers between devices with their start and end apart: 8, of which 5 were waited for; matrix products, arithmetic and copies ran while one was open for 0% of the time, Pallas kernels for 2%

profile of v2, /device:TPU:0, one launch (start us, length us, event | category | flops | bytes accessed | tf_op | source)
XLA Modules:
  0.0 147.6 jit_solution(17375501098961650051)
XLA Ops:
  0.6 1.0 shard_map.87
  1.6 3.1 %collective-permute-start = (f32[8,8,128]{2,1,0:T(8,128)S(1)}, f32[8,8,128]{2,1,0:T(8,128)S(1)}, u32[]{:S(2)}, u32[]{:S(2)}) collective-permute-start(f32[8,8,128]{2,1,0:T(8,128)S(1)} %get-tuple-element.18), channel_id=1, source_target_pairs={{0,8},{8,0},{16,24},{24,16},{1,9},{9,1},{17,25},{25,17},{2,10},{10... | collective-permute-start | bytes 98312 | tf_op jit(solution)/shard_map/ppermute | solution.py:721
  4.7 2.6 %collective-permute-start.1 = (f32[8,8,128]{2,1,0:T(8,128)S(1)}, f32[8,8,128]{2,1,0:T(8,128)S(1)}, u32[]{:S(2)}, u32[]{:S(2)}) collective-permute-start(f32[8,8,128]{2,1,0:T(8,128)S(1)} %get-tuple-element.19), channel_id=1, source_target_pairs={{0,16},{8,24},{16,0},{24,8},{1,17},{9,25},{17,1},{25,9},{2,18},{10... | collective-permute-start | bytes 98312 | tf_op jit(solution)/shard_map/ppermute | solution.py:721
  7.3 0.0 collective-permute-start.2
  7.3 1.8 %shard_map.86 = (f32[8,20,8,128]{3,2,1,0:T(8,128)S(1)}, f32[4,8,128]{2,1,0:T(8,128)S(1)}) custom-call(f32[27,4,8,128]{3,2,1,0:T(8,128)} %refs_0_.3, f32[3,4,8,128]{3,2,1,0:T(8,128)} %refs_1_.2, s32[4,8,128]{2,1,0:T(8,128)} %refs_2_.2), custom_call_target="tpu_custom_call" | custom-call | tf_op jit(solution)/shard_map/pallas_call | solution.py:687
  9.1 0.0 collective-permute-done.refs_3_
  9.1 1.0 collective-permute-done.1.refs_4_
  10.1 2.9 %collective-permute-done.2.refs_5_ = f32[8,8,128]{2,1,0:T(8,128)S(1)} collective-permute-done((f32[8,8,128]{2,1,0:T(8,128)S(1)}, f32[8,8,128]{2,1,0:T(8,128)S(1)}, u32[]{:S(2)}, u32[]{:S(2)}) %collective-permute-start.2) | collective-permute-done | bytes 32800 | tf_op jit(solution)/shard_map/ppermute | solution.py:721
  13.0 0.3 shard_map.88
  13.3 14.7 %all_to_all.10.refs_0_ = f32[8,20,8,128]{3,2,1,0:T(8,128)S(1)} all-to-all(f32[8,20,8,128]{3,2,1,0:T(8,128)S(1)} %shard_map.88), channel_id=1, replica_groups=mesh['grp'=4,'gx'=2,'gy'=4] {'gx','gy'}, dimensions={0} | all-to-all | bytes 1310720 | tf_op jit(solution)/shard_map/all_to_all | solution.py:772
  28.0 2.7 %shard_map.89 = (f32[39,4,8,128]{3,2,1,0:T(8,128)S(1)}, f32[39,2,8,128]{3,2,1,0:T(8,128)S(1)}, f32[39,2,8,128]{3,2,1,0:T(8,128)S(1)}) custom-call(f32[8,20,8,128]{3,2,1,0:T(8,128)S(1)} %all_to_all.10.refs_0_), custom_call_target="tpu_custom_call" | custom-call | tf_op jit(solution)/shard_map/pallas_call | solution.py:687
  30.7 0.1 collective-permute-start.3
  30.8 3.8 %collective-permute-start.4 = (f32[39,2,8,128]{3,2,1,0:T(8,128)S(1)}, f32[39,2,8,128]{3,2,1,0:T(8,128)S(1)}, u32[]{:S(2)}, u32[]{:S(2)}) collective-permute-start(f32[39,2,8,128]{3,2,1,0:T(8,128)S(1)} %get-tuple-element.23), channel_id=1, source_target_pairs={{0,24},{1,0},{2,1},{3,2},{7,3},{6,7},{5,6},{4,5},{12,4},{13,12},{1... | collective-permute-start | bytes 958472 | tf_op jit(solution)/shard_map/ppermute | solution.py:715
  34.6 5.1 %collective-permute-done.3.refs_2_ = f32[39,2,8,128]{3,2,1,0:T(8,128)S(1)} collective-permute-done((f32[39,2,8,128]{3,2,1,0:T(8,128)S(1)}, f32[39,2,8,128]{3,2,1,0:T(8,128)S(1)}, u32[]{:S(2)}, u32[]{:S(2)}) %collective-permute-start.3) | collective-permute-done | bytes 319520 | tf_op jit(solution)/shard_map/ppermute | solution.py:714
  39.7 0.0 collective-permute-done.4.refs_3_
  39.7 84.5 %shard_map.90 = f32[8,17,8,128]{3,2,1,0:T(8,128)S(1)} custom-call(f32[27]{0:T(128)} %refs_0_.5, f32[39,4,8,128]{3,2,1,0:T(8,128)S(1)} %get-tuple-element.21.refs_1_, f32[39,2,8,128]{3,2,1,0:T(8,128)S(1)} %collective-permute-done.3.refs_2_, f32[39,2,8,128]{3,2,1,0:T(8,128)S(1)} %collective-permute-done.4.refs_3_), custom_call_target="tpu_custom_call" | custom-call | tf_op jit(solution)/shard_map/pallas_call | solution.py:687
  124.2 12.5 %all_to_all.11.refs_0_ = f32[8,17,8,128]{3,2,1,0:T(8,128)S(1)} all-to-all(f32[8,17,8,128]{3,2,1,0:T(8,128)S(1)} %shard_map.90), channel_id=1, replica_groups=mesh['grp'=4,'gx'=2,'gy'=4] {'gx','gy'}, dimensions={0} | all-to-all | bytes 1114112 | tf_op jit(solution)/shard_map/all_to_all | solution.py:797
  136.7 0.3 shard_map.92
  136.9 1.2 collective-permute-start.5
  138.2 3.1 %collective-permute-start.6 = (f32[7,8,128]{2,1,0:T(8,128)S(1)}, f32[7,8,128]{2,1,0:T(8,128)S(1)}, u32[]{:S(2)}, u32[]{:S(2)}) collective-permute-start(f32[7,8,128]{2,1,0:T(8,128)S(1)} %get-tuple-element.26), channel_id=1, source_target_pairs={{0,16},{8,24},{16,0},{24,8},{1,17},{9,25},{17,1},{25,9},{2,18},{10... | collective-permute-start | bytes 86024 | tf_op jit(solution)/shard_map/ppermute | solution.py:721
  141.3 0.1 collective-permute-start.7
  141.4 1.9 %shard_map.91 = f32[27,4,8,128]{3,2,1,0:T(8,128)} custom-call(f32[8,17,8,128]{3,2,1,0:T(8,128)S(1)} %all_to_all.11.refs_0_), custom_call_target="tpu_custom_call" | custom-call | tf_op jit(solution)/shard_map/pallas_call | solution.py:687
  143.2 0.0 collective-permute-done.5.refs_1_
  143.2 0.3 collective-permute-done.6.refs_2_
  143.5 3.4 %collective-permute-done.7.refs_3_ = f32[7,8,128]{2,1,0:T(8,128)S(1)} collective-permute-done((f32[7,8,128]{2,1,0:T(8,128)S(1)}, f32[7,8,128]{2,1,0:T(8,128)S(1)}, u32[]{:S(2)}, u32[]{:S(2)}) %collective-permute-start.7) | collective-permute-done | bytes 28704 | tf_op jit(solution)/shard_map/ppermute | solution.py:721
  146.9 0.7 shard_map.93
Async XLA Ops:
  1.6 7.5 %collective-permute-start = (f32[8,8,128]{2,1,0:T(8,128)S(1)}, f32[8,8,128]{2,1,0:T(8,128)S(1)}, u32[]{:S(2)}, u32[]{:S(2)}) collective-permute-start(f32[8,8,128]{2,1,0:T(8,128)S(1)} %get-tuple-element.18), channel_id=1, source_target_pairs={{0,8},{8,0},{16,24},{24,16},{1,9},{9,1},{17,25},{25,17},{2,10},{10... | collective-permute-start | bytes 98312 | tf_op jit(solution)/shard_map/ppermute | solution.py:721
  4.7 5.4 %collective-permute-start.1 = (f32[8,8,128]{2,1,0:T(8,128)S(1)}, f32[8,8,128]{2,1,0:T(8,128)S(1)}, u32[]{:S(2)}, u32[]{:S(2)}) collective-permute-start(f32[8,8,128]{2,1,0:T(8,128)S(1)} %get-tuple-element.19), channel_id=1, source_target_pairs={{0,16},{8,24},{16,0},{24,8},{1,17},{9,25},{17,1},{25,9},{2,18},{10... | collective-permute-start | bytes 98312 | tf_op jit(solution)/shard_map/ppermute | solution.py:721
  7.3 5.7 %collective-permute-start.2 = (f32[8,8,128]{2,1,0:T(8,128)S(1)}, f32[8,8,128]{2,1,0:T(8,128)S(1)}, u32[]{:S(2)}, u32[]{:S(2)}) collective-permute-start(f32[8,8,128]{2,1,0:T(8,128)S(1)} %get-tuple-element.20), channel_id=1, source_target_pairs={{0,24},{8,16},{16,8},{24,0},{1,25},{9,17},{17,9},{25,1},{2,26},{10... | collective-permute-start | bytes 98312 | tf_op jit(solution)/shard_map/ppermute | solution.py:721
  30.7 9.0 %collective-permute-start.3 = (f32[39,2,8,128]{3,2,1,0:T(8,128)S(1)}, f32[39,2,8,128]{3,2,1,0:T(8,128)S(1)}, u32[]{:S(2)}, u32[]{:S(2)}) collective-permute-start(f32[39,2,8,128]{3,2,1,0:T(8,128)S(1)} %get-tuple-element.22), channel_id=1, source_target_pairs={{24,0},{0,1},{1,2},{2,3},{3,7},{7,6},{6,5},{5,4},{4,12},{12,13},{1... | collective-permute-start | bytes 958472 | tf_op jit(solution)/shard_map/ppermute | solution.py:714
  30.8 8.9 %collective-permute-start.4 = (f32[39,2,8,128]{3,2,1,0:T(8,128)S(1)}, f32[39,2,8,128]{3,2,1,0:T(8,128)S(1)}, u32[]{:S(2)}, u32[]{:S(2)}) collective-permute-start(f32[39,2,8,128]{3,2,1,0:T(8,128)S(1)} %get-tuple-element.23), channel_id=1, source_target_pairs={{0,24},{1,0},{2,1},{3,2},{7,3},{6,7},{5,6},{4,5},{12,4},{13,12},{1... | collective-permute-start | bytes 958472 | tf_op jit(solution)/shard_map/ppermute | solution.py:715
  136.9 6.3 %collective-permute-start.5 = (f32[7,8,128]{2,1,0:T(8,128)S(1)}, f32[7,8,128]{2,1,0:T(8,128)S(1)}, u32[]{:S(2)}, u32[]{:S(2)}) collective-permute-start(f32[7,8,128]{2,1,0:T(8,128)S(1)} %get-tuple-element.25), channel_id=1, source_target_pairs={{0,8},{8,0},{16,24},{24,16},{1,9},{9,1},{17,25},{25,17},{2,10},{10... | collective-permute-start | bytes 86024 | tf_op jit(solution)/shard_map/ppermute | solution.py:721
  138.2 5.4 %collective-permute-start.6 = (f32[7,8,128]{2,1,0:T(8,128)S(1)}, f32[7,8,128]{2,1,0:T(8,128)S(1)}, u32[]{:S(2)}, u32[]{:S(2)}) collective-permute-start(f32[7,8,128]{2,1,0:T(8,128)S(1)} %get-tuple-element.26), channel_id=1, source_target_pairs={{0,16},{8,24},{16,0},{24,8},{1,17},{9,25},{17,1},{25,9},{2,18},{10... | collective-permute-start | bytes 86024 | tf_op jit(solution)/shard_map/ppermute | solution.py:721
  141.3 5.7 %collective-permute-start.7 = (f32[7,8,128]{2,1,0:T(8,128)S(1)}, f32[7,8,128]{2,1,0:T(8,128)S(1)}, u32[]{:S(2)}, u32[]{:S(2)}) collective-permute-start(f32[7,8,128]{2,1,0:T(8,128)S(1)} %get-tuple-element.27), channel_id=1, source_target_pairs={{0,24},{8,16},{16,8},{24,0},{1,25},{9,17},{17,9},{25,1},{2,26},{10... | collective-permute-start | bytes 86024 | tf_op jit(solution)/shard_map/ppermute | solution.py:721

commit v3 on v2

--- a/solution.py
+++ b/solution.py
@@ -256,8 +256,9 @@
                 for place in range(self.sub)
             ]
 
-    def holder(self, place, part):
-        return jnp.where(part % 2 == 0, self.snake[place], self.snake[self.sub - 1 - place])
+    def holders(self):
+        even = lax.axis_index("grp") % 2 == 0
+        return [jnp.where(even, *pair) for pair in zip(self.snake, self.snake[::-1])]
 
 
 def lane_index():
@@ -289,19 +290,12 @@
     return values
 
 
-SENT_SPEED, SENT_SOLID, SENT_HEAT, SENT_RATE, SENT = 27, 30, 31, 38, 40
-HEAT_AT, RATE_AT, SPEED_AT, SOLID_AT, ROWS = 27, 34, 35, 38, 39
+SPEED_AT, SOLID_AT, HEAT_AT, RATE_AT, ROWS = 27, 30, 31, 38, 40
 MOVING = 34
 
 
-def row_of(number):
-    if number < SENT_SPEED:
-        return number
-    if number < SENT_SOLID:
-        return SPEED_AT + number - SENT_SPEED
-    if number == SENT_SOLID:
-        return SOLID_AT
-    return HEAT_AT + number - SENT_HEAT if number <= SENT_RATE else None
+def moving_row(number):
+    return number + (HEAT_AT - SPEED_AT) * (number >= SPEED_AT)
 
 
 def offer_heat(slab, levels_hbm, heat_hbm, phase_hbm, *refs):
@@ -328,68 +322,54 @@
         outs[step][7] = 1.0 / (0.5 + 4.0 * chosen)
 
 
-def pack_flow(
-    slab, popul_hbm, speed_hbm, solid_hbm, sent, flags, popul_ref, speed_ref, solid_ref, sems
-):
-    half = 14
+def pack_flow(slab, popul_hbm, speed_hbm, solid_hbm, sent, flags, fields, solid_ref, sems):
     copies = [
-        pltpu.make_async_copy(popul_hbm.at[pl.ds(0, half)], popul_ref.at[pl.ds(0, half)], sems.at[0]),
-        pltpu.make_async_copy(
-            popul_hbm.at[pl.ds(half, 27 - half)], popul_ref.at[pl.ds(half, 27 - half)], sems.at[1]
-        ),
-        pltpu.make_async_copy(speed_hbm, speed_ref, sems.at[2]),
-        pltpu.make_async_copy(solid_hbm, solid_ref, sems.at[3]),
+        pltpu.make_async_copy(popul_hbm, fields.at[pl.ds(0, SPEED_AT)], sems.at[0]),
+        pltpu.make_async_copy(speed_hbm, fields.at[pl.ds(SPEED_AT, 3)], sems.at[1]),
+        pltpu.make_async_copy(solid_hbm, solid_ref, sems.at[2]),
     ]
     for copy in copies:
         copy.start()
-    mine = lax.axis_index("grp")
-    holders = [slab.holder(place, mine) for place in range(slab.sub)]
-
-    def field(number, x):
-        if number < SENT_SPEED:
-            return popul_ref[number, x]
-        return speed_ref[number - SENT_SPEED, x]
-
-    copies[0].wait()
-    for pair in range(SENT_SOLID // 2):
-        if 2 * pair == half:
-            copies[1].wait()
-        if pair == SENT_SPEED // 2:
-            copies[2].wait()
-            copies[3].wait()
-        sources = [field(2 * pair + h, x) for h in range(2) for x in range(slab.block_x)]
-        for place, value in enumerate(swap_groups(sources, slab.planes)):
-            sent[holders[place], pair] = value
-    for x in range(slab.block_x):
-        flags[x] = solid_ref[x].astype(F32)
+    for copy in copies:
+        copy.wait()
+    holders = slab.holders()
+
+    def one(pair, _):
+        pack_pair(slab, fields, pair, sent, pair, holders)
+        return 0
+
+    lax.fori_loop(0, SOLID_AT // 2, one, 0)
+    flags[...] = solid_ref[...].astype(F32)
+
+
+def pack_pair(slab, fields, source, sent, target, holders):
+    sources = [fields[2 * source + h, x] for h in range(2) for x in range(slab.block_x)]
+    for place, value in enumerate(swap_groups(sources, slab.planes)):
+        sent[holders[place], target] = value
 
 
 def pack_heat(slab, sent_in, flags, *refs):
     parts, (sent, held, packed, sem) = refs[: slab.grp], refs[slab.grp :]
     mine = lax.axis_index("grp")
-    holders = [slab.holder(place, mine) for place in range(slab.sub)]
+    holders = slab.holders()
+    held[0] = flags[...]
+    held[9] = jnp.zeros(flags.shape, F32)
     for step in range(slab.grp):
-        held[jnp.bitwise_xor(mine, step)] = parts[step][...]
-    zero = jnp.zeros((SUBLANES, LANES), F32)
-    first = SENT_SOLID // 2
-
-    def field(number, x):
-        if number == SENT_SOLID:
-            return flags[x]
-        return held[x, number - SENT_HEAT] if number <= SENT_RATE else zero
-
-    for pair in range(first, SENT // 2):
-        sources = [field(2 * pair + h, x) for h in range(2) for x in range(slab.block_x)]
-        for place, value in enumerate(swap_groups(sources, slab.planes)):
-            packed[holders[place], pair - first] = value
-    copy = pltpu.make_async_copy(packed, sent.at[:, pl.ds(first, SENT // 2 - first)], sem)
+        held[pl.ds(1, 8), jnp.bitwise_xor(mine, step)] = parts[step][...]
+    first, count = SOLID_AT // 2, (ROWS - SOLID_AT) // 2
+
+    def one(pair, _):
+        pack_pair(slab, held, pair, packed, pair, holders)
+        return 0
+
+    lax.fori_loop(0, count, one, 0)
+    copy = pltpu.make_async_copy(packed, sent.at[:, pl.ds(first, count)], sem)
     copy.start()
     copy.wait()
 
 
 def unpack_in(slab, came, state_out, low_out, high_out):
     half = slab.block_x * slab.planes
-    first_half = lane_index() < half
 
     def put(row, by_gy):
         for tile, value in enumerate(swap_groups(by_gy, slab.deep)):
@@ -399,55 +379,76 @@
             if tile >= slab.tiles - slab.margin:
                 high_out[row, tile - (slab.tiles - slab.margin)] = value
 
-    for pair in range(SENT // 2):
+    def one(pair, _):
+        first_half = lane_index() < half
         firsts, seconds = [], []
         for y in range(slab.gy):
             a, b = came[y, pair], came[slab.gy + y, pair]
             firsts.append(jnp.where(first_half, a, lane_roll(b, half)))
             seconds.append(jnp.where(first_half, lane_roll(a, half), b))
-        put(row_of(2 * pair), firsts)
-        if row_of(2 * pair + 1) is not None:
-            put(row_of(2 * pair + 1), seconds)
+        put(2 * pair, firsts)
+        put(2 * pair + 1, seconds)
+        return 0
+
+    lax.fori_loop(0, ROWS // 2, one, 0)
 
 
 def pack_out(slab, take, sent):
     half = slab.block_x * slab.planes
-    first_half = lane_index() < half
 
     def by_gy(row):
         return swap_groups([take(row, tile) for tile in range(slab.tiles)], slab.deep)
 
-    for pair in range(MOVING // 2):
-        firsts, seconds = by_gy(2 * pair), by_gy(2 * pair + 1)
+    def one(pair, _):
+        first_half = lane_index() < half
+        firsts, seconds = by_gy(moving_row(2 * pair)), by_gy(moving_row(2 * pair + 1))
         for y in range(slab.gy):
             a, b = firsts[y], seconds[y]
             sent[y, pair] = jnp.where(first_half, a, lane_roll(b, half))
             sent[slab.gy + y, pair] = jnp.where(first_half, lane_roll(a, half), b)
-
-
-def unpack_pair(slab, came, pair):
-    mine = lax.axis_index("grp")
-    sources = [came[slab.holder(place, mine), pair] for place in range(slab.sub)]
-    for number, value in enumerate(swap_groups(sources, slab.planes)):
-        yield 2 * pair + number // slab.block_x, number % slab.block_x, value
+        return 0
+
+    lax.fori_loop(0, MOVING // 2, one, 0)
+
+
+def unpack_pair(slab, came, pair, holders):
+    sources = [came[holders[place], pair] for place in range(slab.sub)]
+    values = swap_groups(sources, slab.planes)
+    return [values[: slab.block_x], values[slab.block_x :]]
 
 
 def return_heat(slab, came, *refs):
     outs, held = refs[: slab.grp], refs[slab.grp]
-    for pair in range(HEAT_AT // 2, MOVING // 2):
-        for row, x, value in unpack_pair(slab, came, pair):
-            if row >= HEAT_AT:
-                held[x, row - HEAT_AT] = value
+    holders = slab.holders()
+    _, values = unpack_pair(slab, came, SPEED_AT // 2, holders)
+    for x in range(slab.block_x):
+        held[x, 0] = values[x]
+
+    def one(pair, _):
+        for h, values in enumerate(unpack_pair(slab, came, SPEED_AT // 2 + 1 + pair, holders)):
+            for x in range(slab.block_x):
+                held[x, 2 * pair + 1 + h] = values[x]
+        return 0
+
+    lax.fori_loop(0, 3, one, 0)
     mine = lax.axis_index("grp")
     for step in range(slab.grp):
         outs[step][...] = held[jnp.bitwise_xor(mine, step)]
 
 
 def unpack_flow(slab, came, popul_out):
-    for pair in range((HEAT_AT + 1) // 2):
-        for row, x, value in unpack_pair(slab, came, pair):
-            if row < HEAT_AT:
-                popul_out[row, x] = value
+    holders = slab.holders()
+
+    def one(pair, _):
+        for h, values in enumerate(unpack_pair(slab, came, pair, holders)):
+            for x in range(slab.block_x):
+                popul_out[2 * pair + h, x] = values[x]
+        return 0
+
+    lax.fori_loop(0, SPEED_AT // 2, one, 0)
+    values, _ = unpack_pair(slab, came, SPEED_AT // 2, holders)
+    for x in range(slab.block_x):
+        popul_out[SPEED_AT - 1, x] = values[x]
 
 
 def join_heat(slab, *refs):
@@ -564,10 +565,10 @@
 HEAT_OFFSETS = [(0, 0, 0), (1, 0, 0), (-1, 0, 0), (0, 1, 0), (0, -1, 0), (0, 0, 1), (0, 0, -1)]
 
 
-def run_steps(slab, rates_ref, state, post, force_ref, rate_ref, speed_ref, solid_ref, tiles):
-    def collide_one(tile):
+def run_steps(slab, rates_ref, state, post, force_ref, start, end):
+    def collide_one(tile, _):
         values = [state[n, tile] for n in range(27)]
-        solid = solid_ref[tile] != 0.0
+        solid = state[SOLID_AT, tile] != 0.0
         moved = collide_tile(values, force_ref[tile], lambda n: rates_ref[n])
         for n in range(27):
             post[n, tile] = jnp.where(solid, jnp.nan, moved[n])
@@ -575,21 +576,22 @@
         total = heat[0]
         for k in range(1, 7):
             total = total + heat[k]
-        omega = rate_ref[tile]
+        omega = state[RATE_AT, tile]
         side = 0.125 * total
         half = 0.5 * total
         for k in range(7):
             if k == 0:
                 level = 0.25 * total
             else:
-                drift = half * speed_ref[(k - 1) // 2, tile]
+                drift = half * state[SPEED_AT + (k - 1) // 2, tile]
                 level = side + drift if k % 2 == 1 else side - drift
-            post[HEAT_AT + k, tile] = heat[k] - (heat[k] - level) * omega
-
-    def stream_one(tile, shifts):
-        along_x, along_y, along_z = shifts
-        before, after = max(tile - 1, tiles[0]), min(tile + 1, tiles[-1])
-        solid = solid_ref[tile] != 0.0
+            post[SPEED_AT + k, tile] = heat[k] - (heat[k] - level) * omega
+        return 0
+
+    def stream_one(tile, _):
+        along_x, along_y, along_z = shifters(slab)
+        before, after = jnp.maximum(tile - 1, start), jnp.minimum(tile + 1, end - 1)
+        solid = state[SOLID_AT, tile] != 0.0
 
         def arrive(row, offset):
             value = post[row, tile]
@@ -606,15 +608,12 @@
             value = jnp.where(value != value, post[26 - n, tile], value)
             state[n, tile] = jnp.where(solid, state[n, tile], value)
         for k in range(7):
-            state[HEAT_AT + k, tile] = arrive(HEAT_AT + k, HEAT_OFFSETS[k])
+            state[HEAT_AT + k, tile] = arrive(SPEED_AT + k, HEAT_OFFSETS[k])
+        return 0
 
     def step(number, _):
-        shifts = shifters(slab)
-        for tile in tiles:
-            collide_one(tile)
-            if tile > tiles[0]:
-                stream_one(tile - 1, shifts)
-        stream_one(tiles[-1], shifts)
+        lax.fori_loop(start, end, collide_one, 0)
+        lax.fori_loop(start, end, stream_one, 0)
         return 0
 
     lax.fori_loop(0, STEPS, step, 0)
@@ -647,36 +646,43 @@
 
 
 def both_windows(slab, rates_hbm, own_ref, low_ref, high_ref, *refs):
-    sent, rates_ref, sem, state, post, speed, force, rate_ref, solid_ref = refs
+    sent, rates_ref, sem, state, post, force = refs
     rates_copy = pltpu.make_async_copy(rates_hbm, rates_ref, sem)
     rates_copy.start()
     margin = slab.margin
 
-    def gather(row, tile):
-        if tile < margin:
-            return low_ref[row, tile]
-        if tile >= slab.padded - margin:
-            return high_ref[row, tile - (slab.padded - margin)]
-        return own_ref[row, tile - margin]
-
-    for tile in range(slab.padded):
-        for row in range(MOVING):
-            state[row, tile] = gather(row, tile)
-        for d in range(3):
-            speed[d, tile] = gather(SPEED_AT + d, tile)
-        rate_ref[tile] = gather(RATE_AT, tile)
-        solid_ref[tile] = gather(SOLID_AT, tile)
+    def gather(row, _):
+        state[row, pl.ds(0, margin)] = low_ref[row]
+        state[row, pl.ds(margin, slab.tiles)] = own_ref[row]
+        state[row, pl.ds(slab.padded - margin, margin)] = high_ref[row]
+        return 0
+
+    lax.fori_loop(0, ROWS, gather, 0)
+
+    def first_force(tile, _):
         force[tile] = heat_force(state, tile)
+        return 0
+
+    lax.fori_loop(0, slab.padded, first_force, 0)
     rates_copy.wait()
-    for window in range(WINDOWS):
-        tiles = list(range(window, slab.padded - window))
-        if window > 0:
-            for tile in tiles:
-                solid = solid_ref[tile] != 0.0
-                for d, each in enumerate(flow_speed_tile(state, tile, force[tile])):
-                    speed[d, tile] = jnp.where(solid, 0.0, each)
-                force[tile] = heat_force(state, tile)
-        run_steps(slab, rates_ref, state, post, force, rate_ref, speed, solid_ref, tiles)
+
+    def next_speed(tile, _):
+        solid = state[SOLID_AT, tile] != 0.0
+        for d, each in enumerate(flow_speed_tile(state, tile, force[tile])):
+            state[SPEED_AT + d, tile] = jnp.where(solid, 0.0, each)
+        force[tile] = heat_force(state, tile)
+        return 0
+
+    def one_window(window, _):
+        run_steps(slab, rates_ref, state, post, force, window, slab.padded - window)
+
+        @pl.when(window + 1 < WINDOWS)
+        def _():
+            lax.fori_loop(window + 1, slab.padded - window - 1, next_speed, 0)
+
+        return 0
+
+    lax.fori_loop(0, WINDOWS, one_window, 0)
     pack_out(slab, lambda row, tile: state[row, tile + margin], sent)
 
 
@@ -743,17 +749,16 @@
         in_hbm=3,
     )
     parts = across_planes(slab, parts)
-    sent_shape = (slab.sub, SENT // 2) + tile
+    sent_shape = (slab.sub, ROWS // 2) + tile
     sent, flags = local_call(
         pack_flow,
         slab,
         [populations, velocity_prev, solid],
         [sent_shape, solid.shape],
         [
-            vmem_like(populations),
-            vmem_like(velocity_prev),
-            vmem_like(solid),
-            pltpu.SemaphoreType.DMA((4,)),
+            (SOLID_AT,) + solid.shape,
+            pltpu.VMEM(solid.shape, solid.dtype),
+            pltpu.SemaphoreType.DMA((3,)),
         ],
         in_hbm=3,
     )
@@ -763,8 +768,8 @@
         [sent, flags] + parts,
         [sent_shape],
         [
-            (slab.grp, 8) + tile,
-            (slab.sub, (SENT - SENT_SOLID) // 2) + tile,
+            (ROWS - SOLID_AT,) + solid.shape,
+            (slab.sub, (ROWS - SOLID_AT) // 2) + tile,
             pltpu.SemaphoreType.DMA,
         ],
         carried=True,
@@ -785,11 +790,8 @@
         [
             pltpu.SMEM(rates.shape, F32),
             pltpu.SemaphoreType.DMA,
+            (ROWS, slab.padded) + tile,
             (MOVING, slab.padded) + tile,
-            (MOVING, slab.padded) + tile,
-            (3, slab.padded) + tile,
-            (slab.padded,) + tile,
-            (slab.padded,) + tile,
             (slab.padded,) + tile,
         ],
         in_hbm=1,

time: 148 us -> 90.3 us (0.61)
  Pallas kernels: 93 us -> 39.8 us
  waiting for transfers between devices: 12.7 us -> 7.66 us
    pallas_call x8, Pallas kernels: 93 us -> 39.8 us  [local_call(): pl.pallas_call(kernel, out_shape=[jax.ShapeDtypeStruct(shape, F32) for sh...]
    ppermute x6, waiting for transfers between devices: 7.62 us -> 2.51 us  [across_planes(): lax.ppermute(parts[step], 'grp', [(i, i ^ step) for i in range(slab.grp)])]
  transfers between devices with their start and end apart: 8 -> 8, of which waited for: 5 -> 3; matrix products, arithmetic and copies ran while one was open for 0% -> 0% of each run, Pallas kernels for 2% -> 9%
where the time goes in v3:
time: 90.3 us; the launch traced here: 90 us
  Pallas kernels  39.8 us (44%)
  blocking collectives  27.1 us (30%)
  starting transfers between devices  14.7 us (16%)
  waiting for transfers between devices  7.66 us (8%)
    pallas_call x8, Pallas kernels, local_call(): pl.pallas_call(kernel, out_shape=[jax.ShapeDtypeStruct(shape, F32) for sh...  39.8 us
    all_to_all x2, blocking collectives, on_slabs(): lax.all_to_all(sent, ('gx', 'gy'), split_axis=0, concat_axis=0, tiled=True)  27.1 us
    ppermute x6, starting transfers between devices, across_planes(): lax.ppermute(parts[step], 'grp', [(i, i ^ step) for i in range(slab.grp)])  10.9 us
    ppermute x1, waiting for transfers between devices, exchange(): from_below = lax.ppermute(high, RING, upward)  5.15 us
    ppermute x1, starting transfers between devices, exchange(): from_above = lax.ppermute(low, RING, [(b, a) for a, b in upward])  3.81 us
    ppermute x6, waiting for transfers between devices, across_planes(): lax.ppermute(parts[step], 'grp', [(i, i ^ step) for i in range(slab.grp)])  2.51 us
  transfers between devices with their start and end apart: 8, of which 3 were waited for; matrix products, arithmetic and copies ran while one was open for 0% of the time, Pallas kernels for 9%

profile of v3, /device:TPU:0, one launch (start us, length us, event | category | flops | bytes accessed | tf_op | source)
XLA Modules:
  0.0 90.0 jit_solution(14300368553688784077)
XLA Ops:
  0.6 1.0 %shard_map.87 = (f32[8,8,128]{2,1,0:T(8,128)S(1)}, f32[8,8,128]{2,1,0:T(8,128)S(1)}, f32[8,8,128]{2,1,0:T(8,128)S(1)}, f32[8,8,128]{2,1,0:T(8,128)S(1)}) custom-call(f32[4]{0:T(128)} %refs_0_.4, f32[7,1,8,512]{3,2,1,0:T(8,128)} %refs_1_.3, s32[1,8,512]{2,1,0:T(8,128)} %refs_2_.3), custom_call_target="tpu_custom_call" | custom-call | tf_op jit(solution)/shard_map/pallas_call | solution.py:693
  1.6 3.1 %collective-permute-start = (f32[8,8,128]{2,1,0:T(8,128)S(1)}, f32[8,8,128]{2,1,0:T(8,128)S(1)}, u32[]{:S(2)}, u32[]{:S(2)}) collective-permute-start(f32[8,8,128]{2,1,0:T(8,128)S(1)} %get-tuple-element.18), channel_id=1, source_target_pairs={{0,8},{8,0},{16,24},{24,16},{1,9},{9,1},{17,25},{25,17},{2,10},{10... | collective-permute-start | bytes 98312 | tf_op jit(solution)/shard_map/ppermute | solution.py:727
  4.7 2.6 %collective-permute-start.1 = (f32[8,8,128]{2,1,0:T(8,128)S(1)}, f32[8,8,128]{2,1,0:T(8,128)S(1)}, u32[]{:S(2)}, u32[]{:S(2)}) collective-permute-start(f32[8,8,128]{2,1,0:T(8,128)S(1)} %get-tuple-element.19), channel_id=1, source_target_pairs={{0,16},{8,24},{16,0},{24,8},{1,17},{9,25},{17,1},{25,9},{2,18},{10... | collective-permute-start | bytes 98312 | tf_op jit(solution)/shard_map/ppermute | solution.py:727
  7.3 0.0 collective-permute-start.2
  7.3 4.3 %shard_map.86 = (f32[8,20,8,128]{3,2,1,0:T(8,128)S(1)}, f32[4,8,128]{2,1,0:T(8,128)S(1)}) custom-call(f32[27,4,8,128]{3,2,1,0:T(8,128)} %refs_0_.3, f32[3,4,8,128]{3,2,1,0:T(8,128)} %refs_1_.2, s32[4,8,128]{2,1,0:T(8,128)} %refs_2_.2), custom_call_target="tpu_custom_call" | custom-call | tf_op jit(solution)/shard_map/pallas_call | solution.py:693
  11.6 0.0 collective-permute-done.refs_3_
  11.6 0.0 collective-permute-done.1.refs_4_
  11.6 1.4 %collective-permute-done.2.refs_5_ = f32[8,8,128]{2,1,0:T(8,128)S(1)} collective-permute-done((f32[8,8,128]{2,1,0:T(8,128)S(1)}, f32[8,8,128]{2,1,0:T(8,128)S(1)}, u32[]{:S(2)}, u32[]{:S(2)}) %collective-permute-start.2) | collective-permute-done | bytes 32800 | tf_op jit(solution)/shard_map/ppermute | solution.py:727
  13.0 1.1 %shard_map.88 = f32[8,20,8,128]{3,2,1,0:T(8,128)S(1)} custom-call(f32[8,20,8,128]{3,2,1,0:T(8,128)S(1)} %get-tuple-element.15.refs_0_, f32[4,8,128]{2,1,0:T(8,128)S(1)} %get-tuple-element.16.refs_1_, f32[8,8,128]{2,1,0:T(8,128)S(1)} %get-tuple-element.17.refs_2_, f32[8,8,128]{2,1,0:T(8,128)S(1)} %collective-permute-done.refs_3_, ...), custom_call_target="tpu_custom_call", output_to_operand_aliasing={{}: (0, {})} | custom-call | tf_op jit(solution)/shard_map/pallas_call | solution.py:693
  14.1 14.7 %all_to_all.10.refs_0_ = f32[8,20,8,128]{3,2,1,0:T(8,128)S(1)} all-to-all(f32[8,20,8,128]{3,2,1,0:T(8,128)S(1)} %shard_map.88), channel_id=1, replica_groups=mesh['grp'=4,'gx'=2,'gy'=4] {'gx','gy'}, dimensions={0} | all-to-all | bytes 1310720 | tf_op jit(solution)/shard_map/all_to_all | solution.py:777
  28.8 4.4 %shard_map.89 = (f32[40,4,8,128]{3,2,1,0:T(8,128)S(1)}, f32[40,2,8,128]{3,2,1,0:T(8,128)S(1)}, f32[40,2,8,128]{3,2,1,0:T(8,128)S(1)}) custom-call(f32[8,20,8,128]{3,2,1,0:T(8,128)S(1)} %all_to_all.10.refs_0_), custom_call_target="tpu_custom_call" | custom-call | tf_op jit(solution)/shard_map/pallas_call | solution.py:693
  33.2 0.1 collective-permute-start.3
  33.3 3.8 %collective-permute-start.4 = (f32[40,2,8,128]{3,2,1,0:T(8,128)S(1)}, f32[40,2,8,128]{3,2,1,0:T(8,128)S(1)}, u32[]{:S(2)}, u32[]{:S(2)}) collective-permute-start(f32[40,2,8,128]{3,2,1,0:T(8,128)S(1)} %get-tuple-element.23), channel_id=1, source_target_pairs={{0,24},{1,0},{2,1},{3,2},{7,3},{6,7},{5,6},{4,5},{12,4},{13,12},{1... | collective-permute-start | bytes 983048 | tf_op jit(solution)/shard_map/ppermute | solution.py:721
  37.1 5.2 %collective-permute-done.3.refs_2_ = f32[40,2,8,128]{3,2,1,0:T(8,128)S(1)} collective-permute-done((f32[40,2,8,128]{3,2,1,0:T(8,128)S(1)}, f32[40,2,8,128]{3,2,1,0:T(8,128)S(1)}, u32[]{:S(2)}, u32[]{:S(2)}) %collective-permute-start.3) | collective-permute-done | bytes 327712 | tf_op jit(solution)/shard_map/ppermute | solution.py:720
  42.2 0.0 collective-permute-done.4.refs_3_
  42.2 23.7 %shard_map.90 = f32[8,17,8,128]{3,2,1,0:T(8,128)S(1)} custom-call(f32[27]{0:T(128)} %refs_0_.5, f32[40,4,8,128]{3,2,1,0:T(8,128)S(1)} %get-tuple-element.21.refs_1_, f32[40,2,8,128]{3,2,1,0:T(8,128)S(1)} %collective-permute-done.3.refs_2_, f32[40,2,8,128]{3,2,1,0:T(8,128)S(1)} %collective-permute-done.4.refs_3_), custom_call_target="tpu_custom_call" | custom-call | tf_op jit(solution)/shard_map/pallas_call | solution.py:693
  66.0 12.5 %all_to_all.11.refs_0_ = f32[8,17,8,128]{3,2,1,0:T(8,128)S(1)} all-to-all(f32[8,17,8,128]{3,2,1,0:T(8,128)S(1)} %shard_map.90), channel_id=1, replica_groups=mesh['grp'=4,'gx'=2,'gy'=4] {'gx','gy'}, dimensions={0} | all-to-all | bytes 1114112 | tf_op jit(solution)/shard_map/all_to_all | solution.py:799
  78.5 0.9 shard_map.92
  79.3 2.7 %collective-permute-start.5 = (f32[7,8,128]{2,1,0:T(8,128)S(1)}, f32[7,8,128]{2,1,0:T(8,128)S(1)}, u32[]{:S(2)}, u32[]{:S(2)}) collective-permute-start(f32[7,8,128]{2,1,0:T(8,128)S(1)} %get-tuple-element.25), channel_id=1, source_target_pairs={{0,8},{8,0},{16,24},{24,16},{1,9},{9,1},{17,25},{25,17},{2,10},{10... | collective-permute-start | bytes 86024 | tf_op jit(solution)/shard_map/ppermute | solution.py:727
  82.1 1.6 %collective-permute-start.6 = (f32[7,8,128]{2,1,0:T(8,128)S(1)}, f32[7,8,128]{2,1,0:T(8,128)S(1)}, u32[]{:S(2)}, u32[]{:S(2)}) collective-permute-start(f32[7,8,128]{2,1,0:T(8,128)S(1)} %get-tuple-element.26), channel_id=1, source_target_pairs={{0,16},{8,24},{16,0},{24,8},{1,17},{9,25},{17,1},{25,9},{2,18},{10... | collective-permute-start | bytes 86024 | tf_op jit(solution)/shard_map/ppermute | solution.py:727
  83.7 0.8 collective-permute-start.7
  84.5 3.8 %shard_map.91 = f32[27,4,8,128]{3,2,1,0:T(8,128)} custom-call(f32[8,17,8,128]{3,2,1,0:T(8,128)S(1)} %all_to_all.11.refs_0_), custom_call_target="tpu_custom_call" | custom-call | tf_op jit(solution)/shard_map/pallas_call | solution.py:693
  88.3 0.0 collective-permute-done.5.refs_1_
  88.3 0.0 collective-permute-done.6.refs_2_
  88.3 1.1 %collective-permute-done.7.refs_3_ = f32[7,8,128]{2,1,0:T(8,128)S(1)} collective-permute-done((f32[7,8,128]{2,1,0:T(8,128)S(1)}, f32[7,8,128]{2,1,0:T(8,128)S(1)}, u32[]{:S(2)}, u32[]{:S(2)}) %collective-permute-start.7) | collective-permute-done | bytes 28704 | tf_op jit(solution)/shard_map/ppermute | solution.py:727
  89.4 0.7 shard_map.93
Async XLA Ops:
  1.6 9.9 %collective-permute-start = (f32[8,8,128]{2,1,0:T(8,128)S(1)}, f32[8,8,128]{2,1,0:T(8,128)S(1)}, u32[]{:S(2)}, u32[]{:S(2)}) collective-permute-start(f32[8,8,128]{2,1,0:T(8,128)S(1)} %get-tuple-element.18), channel_id=1, source_target_pairs={{0,8},{8,0},{16,24},{24,16},{1,9},{9,1},{17,25},{25,17},{2,10},{10... | collective-permute-start | bytes 98312 | tf_op jit(solution)/shard_map/ppermute | solution.py:727
  4.7 6.9 %collective-permute-start.1 = (f32[8,8,128]{2,1,0:T(8,128)S(1)}, f32[8,8,128]{2,1,0:T(8,128)S(1)}, u32[]{:S(2)}, u32[]{:S(2)}) collective-permute-start(f32[8,8,128]{2,1,0:T(8,128)S(1)} %get-tuple-element.19), channel_id=1, source_target_pairs={{0,16},{8,24},{16,0},{24,8},{1,17},{9,25},{17,1},{25,9},{2,18},{10... | collective-permute-start | bytes 98312 | tf_op jit(solution)/shard_map/ppermute | solution.py:727
  7.3 5.7 %collective-permute-start.2 = (f32[8,8,128]{2,1,0:T(8,128)S(1)}, f32[8,8,128]{2,1,0:T(8,128)S(1)}, u32[]{:S(2)}, u32[]{:S(2)}) collective-permute-start(f32[8,8,128]{2,1,0:T(8,128)S(1)} %get-tuple-element.20), channel_id=1, source_target_pairs={{0,24},{8,16},{16,8},{24,0},{1,25},{9,17},{17,9},{25,1},{2,26},{10... | collective-permute-start | bytes 98312 | tf_op jit(solution)/shard_map/ppermute | solution.py:727
  33.2 9.0 %collective-permute-start.3 = (f32[40,2,8,128]{3,2,1,0:T(8,128)S(1)}, f32[40,2,8,128]{3,2,1,0:T(8,128)S(1)}, u32[]{:S(2)}, u32[]{:S(2)}) collective-permute-start(f32[40,2,8,128]{3,2,1,0:T(8,128)S(1)} %get-tuple-element.22), channel_id=1, source_target_pairs={{24,0},{0,1},{1,2},{2,3},{3,7},{7,6},{6,5},{5,4},{4,12},{12,13},{1... | collective-permute-start | bytes 983048 | tf_op jit(solution)/shard_map/ppermute | solution.py:720
  33.3 9.0 %collective-permute-start.4 = (f32[40,2,8,128]{3,2,1,0:T(8,128)S(1)}, f32[40,2,8,128]{3,2,1,0:T(8,128)S(1)}, u32[]{:S(2)}, u32[]{:S(2)}) collective-permute-start(f32[40,2,8,128]{3,2,1,0:T(8,128)S(1)} %get-tuple-element.23), channel_id=1, source_target_pairs={{0,24},{1,0},{2,1},{3,2},{7,3},{6,7},{5,6},{4,5},{12,4},{13,12},{1... | collective-permute-start | bytes 983048 | tf_op jit(solution)/shard_map/ppermute | solution.py:721
  79.3 8.9 %collective-permute-start.5 = (f32[7,8,128]{2,1,0:T(8,128)S(1)}, f32[7,8,128]{2,1,0:T(8,128)S(1)}, u32[]{:S(2)}, u32[]{:S(2)}) collective-permute-start(f32[7,8,128]{2,1,0:T(8,128)S(1)} %get-tuple-element.25), channel_id=1, source_target_pairs={{0,8},{8,0},{16,24},{24,16},{1,9},{9,1},{17,25},{25,17},{2,10},{10... | collective-permute-start | bytes 86024 | tf_op jit(solution)/shard_map/ppermute | solution.py:727
  82.1 6.2 %collective-permute-start.6 = (f32[7,8,128]{2,1,0:T(8,128)S(1)}, f32[7,8,128]{2,1,0:T(8,128)S(1)}, u32[]{:S(2)}, u32[]{:S(2)}) collective-permute-start(f32[7,8,128]{2,1,0:T(8,128)S(1)} %get-tuple-element.26), channel_id=1, source_target_pairs={{0,16},{8,24},{16,0},{24,8},{1,17},{9,25},{17,1},{25,9},{2,18},{10... | collective-permute-start | bytes 86024 | tf_op jit(solution)/shard_map/ppermute | solution.py:727
  83.7 5.7 %collective-permute-start.7 = (f32[7,8,128]{2,1,0:T(8,128)S(1)}, f32[7,8,128]{2,1,0:T(8,128)S(1)}, u32[]{:S(2)}, u32[]{:S(2)}) collective-permute-start(f32[7,8,128]{2,1,0:T(8,128)S(1)} %get-tuple-element.27), channel_id=1, source_target_pairs={{0,24},{8,16},{16,8},{24,0},{1,25},{9,17},{17,9},{25,1},{2,26},{10... | collective-permute-start | bytes 86024 | tf_op jit(solution)/shard_map/ppermute | solution.py:727
